TPU v7x, 1024 devices: a whole 4x8x16 slice. The times are simulated.
1024 devices in a mesh: angle: 32 (over x_lo, y, core), scan: 32 (over z, x_hi).
Axes of the slice: x: 4 (x_hi: 2, x_lo: 2; x = x_hi * 2 + x_lo), y: 8, z: 16, core: 2. Of those that a mesh axis runs over, the one named last changes fastest.
Arguments:
- object_slices: float32 [2, 3, 2048, 512], P(None, None, 'scan', 'angle'), may hold values from -5 to 5
- probe: float32 [2, 128, 128], replicated, may hold values from -6 to 6
- intensities: float32 [32, 32, 2, 128, 128], P('angle', 'scan'), may hold values from 0.5 to 3.5
- row_offsets: int32 [32, 32, 2], P('angle', 'scan'), may hold values from 0 to 64
- column_starts: int32 [32, 32, 2], P('angle', 'scan'), may hold values from 0 to 320
- slice_shifts: int32 [32, 3], P('angle'), may hold values from 0 to 64
- counts: int32 [32, 32], P('angle', 'scan'), may hold values from 1 to 2, as said below
Outputs:
- object_gradient: float32 [2, 3, 2048, 512], P(None, None, 'scan', 'angle')
- probe_gradient: float32 [2, 128, 128], replicated
Inputs may be any that keep to these rules, and one draw needn't show every extreme that they name: `counts`: the largest value 2 occurs in every draw.
All inputs are finite; a program needn't handle non-finite values.
Results may differ from a plain program's by a relative error of at most 0.0003.
Values sent between devices are 32-bit elements; how exact they have to be, the bound alone decides.
No kernel may reach another device: no remote copies, remote signals or barrier semaphores. Data moves between devices by JAX's collectives and lax.ppermute only.
A program may use at most 32 MiB of HBM per device.

v0:
```python
from functools import partial

import jax
import jax.numpy as jnp
from jax import lax
from jax.sharding import PartitionSpec as P


def padded(cells, sides, width):
    for axis, dim in sides:
        count = lax.axis_size(axis)
        ends = count - 1
        head = lax.slice_in_dim(cells, 0, width, axis=dim)
        tail = lax.slice_in_dim(cells, cells.shape[dim] - width, cells.shape[dim], axis=dim)
        cells = jnp.concatenate(
            [
                lax.ppermute(tail, axis, [(i, (i + 1) % count) for i in range(ends)]),
                cells,
                lax.ppermute(head, axis, [((i + 1) % count, i) for i in range(ends)]),
            ],
            axis=dim,
        )
    return cells


def cut_along(array, dim, length):
    before, after = (array.shape[:dim], array.shape[dim + 1 :])
    return jnp.moveaxis(array.reshape(*before, length, -1, *after), dim, 0)


def summed_on_arrival(array, axis, dim):
    length = lax.axis_size(axis)
    blocks = lax.all_to_all(cut_along(array, dim, length), axis, 0, 0, tiled=True)
    return jnp.sum(blocks, axis=0)


def over_pieces(array, axis):
    blocks = lax.all_gather(array, axis)
    return blocks.sum(axis=0)


def propagator(size):
    index = jnp.arange(size, dtype=jnp.int32)
    centred = ((index + size // 2) % size - size // 2).astype(jnp.float32)
    radius = centred[:, None] * centred[:, None] + centred[None, :] * centred[None, :]
    phase = 8.0 * jnp.pi * radius / (size * size)
    return (jnp.cos(phase), jnp.sin(phase))


def tables(size):
    index = jnp.arange(size, dtype=jnp.int32)
    turns = index[:, None] * index[None, :] % size
    phase = 2.0 * jnp.pi * turns.astype(jnp.float32) / size
    scale = 1.0 / jnp.sqrt(jnp.float32(size))
    return (jnp.cos(phase) * scale, jnp.sin(phase) * scale)


def matmul(first, second):
    return jnp.dot(
        first, second, precision=lax.Precision.HIGHEST, preferred_element_type=jnp.float32
    )


def transform(real_part, imag_part, cosine, sine, sign):
    left_re = matmul(cosine, real_part) - sign * matmul(sine, imag_part)
    left_im = matmul(cosine, imag_part) + sign * matmul(sine, real_part)
    right_re = matmul(left_re, cosine) - sign * matmul(left_im, sine)
    right_im = matmul(left_im, cosine) + sign * matmul(left_re, sine)
    return (right_re, right_im)


def local_loss(slab, probe, measured, weight, cosine, sine, kern_re, kern_im):
    wave_re, wave_im = (probe[0], probe[1])
    layers = slab.shape[1]
    for k in range(layers):
        object_re, object_im = (slab[0, k], slab[1, k])
        wave_re, wave_im = (
            wave_re * object_re - wave_im * object_im,
            wave_re * object_im + wave_im * object_re,
        )
        if k + 1 < layers:
            freq_re, freq_im = transform(wave_re, wave_im, cosine, sine, -1.0)
            freq_re, freq_im = (
                freq_re * kern_re - freq_im * kern_im,
                freq_re * kern_im + freq_im * kern_re,
            )
            wave_re, wave_im = transform(freq_re, freq_im, cosine, sine, 1.0)
    far_re, far_im = transform(wave_re, wave_im, cosine, sine, -1.0)
    differ = far_re * far_re + far_im * far_im - measured
    return weight * jnp.sum(differ * differ)


def local(object_slices, probe, intensities, row_offsets, column_starts, slice_shifts, counts):
    band = object_slices.shape[2]
    framed = padded(object_slices, (("scan", 2),), band)
    region = lax.all_gather(framed, "angle", axis=3, tiled=True)
    size = probe.shape[1]
    slots = row_offsets.shape[2]
    layers = region.shape[1]
    angles = lax.axis_size("angle")
    cosine, sine = tables(size)
    kern_re, kern_im = propagator(size)
    shifts = slice_shifts[0]
    zero = jnp.zeros((), jnp.int32)

    def visit(slot, carry):
        gradient_region, gradient_probe = carry
        top = row_offsets[0, 0, slot]
        start = column_starts[0, 0, slot]
        slab = jnp.concatenate(
            [
                lax.dynamic_slice(
                    region, (zero, zero + k, top, start + shifts[k]), (2, 1, size, size)
                )
                for k in range(layers)
            ],
            axis=1,
        )
        weight = jnp.where(slot < counts[0, 0], 0.5 / angles, 0.0).astype(jnp.float32)
        measured = intensities[0, 0, slot]
        scorer = partial(
            local_loss,
            measured=measured,
            weight=weight,
            cosine=cosine,
            sine=sine,
            kern_re=kern_re,
            kern_im=kern_im,
        )
        loss, pull = jax.vjp(scorer, slab, probe)
        slab_grad, probe_grad = pull(jnp.ones_like(loss))
        for k in range(layers):
            place = (zero, zero + k, top, start + shifts[k])
            current = lax.dynamic_slice(gradient_region, place, (2, 1, size, size))
            gradient_region = lax.dynamic_update_slice(
                gradient_region, current + slab_grad[:, k : k + 1], place
            )
        return (gradient_region, gradient_probe + probe_grad)

    start_carry = (jnp.zeros(region.shape, jnp.float32), jnp.zeros(probe.shape, jnp.float32))
    gradient_region, gradient_probe = lax.fori_loop(0, slots, visit, start_carry)
    shared = summed_on_arrival(gradient_region, "angle", 3)
    edges = jnp.concatenate([shared[:, :, :band], shared[:, :, 2 * band :]], axis=2)
    rimmed = padded(edges, (("scan", 2),), band)
    object_gradient = shared[:, :, band : 2 * band] + rimmed[:, :, :band] + rimmed[:, :, 3 * band :]
    group_total = over_pieces(gradient_probe, "scan")
    probe_gradient = over_pieces(group_total, "angle")
    return (object_gradient, probe_gradient)


def solution(mesh):
    return jax.shard_map(
        local,
        mesh=mesh,
        in_specs=(
            P(None, None, "scan", "angle"),
            P(),
            P("angle", "scan", None, None, None),
            P("angle", "scan", None),
            P("angle", "scan", None),
            P("angle", None),
            P("angle", "scan"),
        ),
        out_specs=(P(None, None, "scan", "angle"), P()),
        check_vma=False,
    )
```

profile of v0, /device:TPU:1, one launch (start us, length us, event | category | flops | bytes accessed | tf_op | source)
XLA Modules:
  0.0 550.2 jit_solution(8382604395229700524)
XLA Ops:
  7.2 5.5 collective-permute-start
  14.2 5.1 collective-permute-done.1
  21.0 84.6 %all-gather.6.cloned.1.call-done = f32[2,3,192,512]{2,0,1,3:T(2,128)} async-done(((f32[2,3,192,16]{2,0,1,3:T(2,128)}), f32[2,3,192,512]{2,0,1,3:T(2,128)}) %all-gather.6.cloned.1.call-update) | async-done | bytes 2359312 | tf_op jit(solution)/shard_map/all_gather | solution.py:96
  105.5 5.5 %copy.41 = f32[2,3,192,512]{3,2,1,0:T(8,128)} copy(f32[2,3,192,512]{2,0,1,3:T(2,128)} %all-gather.6.cloned.1.call-done) | data formatting | bytes 4718592
  112.1 136.2 %while.19 = (s32[]{:T(128)}, f32[2,3,192,512]{3,2,1,0:T(8,128)S(1)}, f32[2,128,128]{2,1,0:T(8,128)S(1)}, s32[1,1,2]{2,1,0:T(1,128)S(1)}, s32[1,1,2]{2,1,0:T(1,12...) while((s32[]{:T(128)}, ...), condition=%wide.region_1.2_spmd.clone.clone.clone.clone, body=%wide.region_0.1_spmd.clone.clone.clone.clone.sunk | while | flops 2037301248 | bytes 20128300 | solution.py:141
  129.6 1.5 multiply_add_fusion.7
  135.8 1.3 convolution_add_fusion.37
  140.2 1.5 multiply_subtract_fusion.3
  149.2 1.5 add_bitcast_fusion.9
  159.8 1.5 add_bitcast_fusion.10
  170.4 1.5 add_bitcast_fusion.11
  172.1 2.2 dynamic_update_slice.36
  174.4 2.2 dynamic_update_slice.37
  176.8 2.2 dynamic_update_slice.38
  196.8 1.5 multiply_add_fusion.7
  207.0 1.5 multiply_subtract_fusion.3
  216.1 1.5 add_bitcast_fusion.9
  226.7 1.5 add_bitcast_fusion.10
  237.4 1.5 add_bitcast_fusion.11
  239.2 2.1 dynamic_update_slice.36
  241.4 2.1 dynamic_update_slice.37
  243.7 2.1 dynamic_update_slice.38
  249.1 162.2 %all-gather.8.cloned.1.call-done = f32[64,128,128]{2,1,0:T(8,128)} async-done(((f32[2,128,128]{2,1,0:T(8,128)}), f32[64,128,128]{2,1,0:T(8,128)}) %all-gather.8.cloned.1.call-update) | async-done | bytes 4194320 | tf_op jit(solution)/shard_map/all_gather | solution.py:38
  411.3 3.0 reduce_sum.28
  414.3 2.3 copy.42
  416.7 2.2 copy.43
  418.9 108.5 %all_to_all.5 = f32[32,2,3,192,16]{3,4,2,1,0:T(8,128)} all-to-all(f32[32,2,3,192,16]{3,4,2,1,0:T(8,128)S(1)} %copy.43), channel_id=1, replica_groups=mesh['angle'=32,'scan'=32] {'angle'}, dimensions={0} | all-to-all | bytes 4718592 | tf_op jit(solution)/shard_map/all_to_all | solution.py:33
  527.4 2.2 reduce_sum.27
  529.6 3.8 collective-permute-start.2
  533.4 1.3 collective-permute-start.3
  534.7 5.0 collective-permute-done.3
  540.4 3.0 reduce_sum.29
  (194 shorter events, 95.8 us)
Async XLA Ops:
  7.2 98.4 %all-gather.6.cloned.1.call-start = ((), (), s32[]{:S(2)}) async-start(), calls=%async_computation.1 | async-start | bytes 3244032 | tf_op jit(solution)/shard_map/all_gather | solution.py:96
  7.2 7.0 %collective-permute-start = (f32[2,3,64,16]{2,3,1,0:T(8,128)}, f32[2,3,64,16]{2,3,1,0:T(8,128)S(1)}, u32[]{:S(2)}, u32[]{:S(2)}) collective-permute-start(f32[2,3,64,16]{2,3,1,0:T(8,128)} %param.9), channel_id=1, source_target_pairs={{0,1},{1,2},{2,3},{3,4},{4,5},{5,6},{6,7},{7,8},{8,9},{9,10},{10,1... | collective-permute-start | bytes 73736 | tf_op jit(solution)/shard_map/ppermute | solution.py:17
  12.7 6.5 %collective-permute-start.1 = (f32[2,3,64,16]{2,3,1,0:T(8,128)}, f32[2,3,64,16]{2,3,1,0:T(8,128)S(1)}, u32[]{:S(2)}, u32[]{:S(2)}) collective-permute-start(f32[2,3,64,16]{2,3,1,0:T(8,128)} %param.9), channel_id=1, source_target_pairs={{1,0},{2,1},{3,2},{4,3},{5,4},{6,5},{7,6},{8,7},{9,8},{10,9},{11,1... | collective-permute-start | bytes 73736 | tf_op jit(solution)/shard_map/ppermute | solution.py:19
  20.9 390.4 %all-gather.8.cloned.1.call-start = ((), (), s32[]{:S(2)}) async-start(), calls=%async_computation.2 | async-start | bytes 4325376 | tf_op jit(solution)/shard_map/all_gather | solution.py:38
  111.1 0.9 copy-start
  111.1 0.9 copy-start.2
  111.1 0.9 copy-start.3
  111.1 0.9 copy-start.4
  111.1 1.0 copy-start.5
  248.3 0.7 copy-start.1
  249.0 291.4 %all-gather.10.cloned.1.call-start = ((), (), s32[]{:S(2)}) async-start(), calls=%async_computation.3 | async-start | bytes 4325376 | tf_op jit(solution)/shard_map/all_gather | solution.py:38
  529.6 5.1 collective-permute-start.2
  533.4 6.3 %collective-permute-start.3 = (f32[2,3,64,16]{2,3,1,0:T(8,128)S(1)}, f32[2,3,64,16]{2,3,1,0:T(8,128)S(1)}, u32[]{:S(2)}, u32[]{:S(2)}) collective-permute-start(f32[2,3,64,16]{2,3,1,0:T(8,128)S(1)} %get-tuple-element.812), channel_id=1, source_target_pairs={{1,0},{2,1},{3,2},{4,3},{5,4},{6,5},{7,6},{8,7},{9,8},{10,9},{11,1... | collective-permute-start | bytes 73736 | tf_op jit(solution)/shard_map/ppermute | solution.py:19
Sparse Core Ops, SparseCore 0:
  21.0 84.4 all-gather.5
  249.1 162.0 all-gather.7
  414.6 111.0 all-gather.9
where the time goes:
time: 556 us; the launch traced here: 550 us
  waiting for transfers between devices  257 us (46%)
  blocking collectives  108 us (19%)
  matrix products  101 us (18%)
  local copies, waits for them, and re-layouts  28.1 us (5%)
  loops' own time  16.7 us (3%)
  between operations  14.1 us (3%)
  other arithmetic  12.9 us (2%)
  starting transfers between devices  12 us (2%)
    all_gather x2, waiting for transfers between devices, over_pieces(): blocks = lax.all_gather(array, axis)  162 us
    all_to_all x1, blocking collectives, summed_on_arrival(): lax.all_to_all(cut_along(array, dim, length), axis, 0, 0, tiled=True)  108 us
    dot_general x160, matrix products, matmul(): jnp.dot(first, second, precision=lax.Precision.HIGHEST, preferred_element...  101 us
    all_gather x1, waiting for transfers between devices, local(): region = lax.all_gather(framed, 'angle', axis=3, tiled=True)  84.6 us
    another operation x1, loops' own time, local(): lax.fori_loop(0, slots, visit, start_carry)  16.7 us
    dynamic_update_slice x6, local copies, waits for them, and re-layouts, visit(): lax.dynamic_update_slice(gradient_region, current + slab_grad[:, k:k + 1]...  13.1 us
  transfers between devices with their start and end apart: 7, of which 5 were waited for; matrix products, arithmetic and copies ran while one was open for 1% of the time, Pallas kernels for 0%

commit v1 on v0

v1 whole, which is shorter than its diff:
```python
import jax
import jax.numpy as jnp
import numpy as np
from jax import lax
from jax.experimental import pallas as pl
from jax.experimental.pallas import tpu as pltpu
from jax.sharding import Mesh
from jax.sharding import PartitionSpec as P

PLANE = ("xl", "y")
ANGLE = ("xl", "y", "c")
SCAN = ("z", "xh")
ANY = pl.BlockSpec(memory_space=pl.ANY)
VMEM = pl.BlockSpec(memory_space=pltpu.VMEM)
SMEM = pl.BlockSpec(memory_space=pltpu.SMEM)


def tables(size):
    index = np.arange(size)
    centred = ((index + size // 2) % size - size // 2).astype(np.float64)
    dft = np.exp(-2j * np.pi * (np.outer(index, index) % size) / size) / np.sqrt(size)
    step = dft.conj() @ (np.exp(8j * np.pi * centred * centred / size**2)[:, None] * dft)
    out = []
    for m in (0.5 * (step + step.T), dft):
        left = np.block([[m.real, -m.imag], [m.imag, m.real]])
        right = np.block([[m.real, m.imag], [-m.imag, m.real]])
        for block, axis in ((left, 1), (right, 0)):
            block = block.astype(np.float32)
            high = block.astype(jnp.bfloat16)
            low = (block - high.astype(np.float32)).astype(jnp.bfloat16)
            out.append(np.concatenate([high, low, high], axis=axis))
    return out


def parts(x, axis):
    high = x.astype(jnp.bfloat16)
    low = (x - high.astype(jnp.float32)).astype(jnp.bfloat16)
    return jnp.concatenate([high, high, low], axis=axis)


def two_sided(values, left, right):
    n = len(values)
    size = values[0][0].shape[0]
    stack = jnp.concatenate(
        [jnp.concatenate([v[i] for v in values], axis=1) for i in range(2)], axis=0
    )
    y = jnp.dot(left, parts(stack, 0), preferred_element_type=jnp.float32)
    rows = jnp.concatenate(
        [
            jnp.concatenate([y[i * size : (i + 1) * size, p * size : (p + 1) * size] for i in range(2)], axis=1)
            for p in range(n)
        ],
        axis=0,
    )
    z = jnp.dot(parts(rows, 1), right, preferred_element_type=jnp.float32)
    return [(z[p * size : (p + 1) * size, :size], z[p * size : (p + 1) * size, size:]) for p in range(n)]


def product(a, b):
    return (a[0] * b[0] - a[1] * b[1], a[0] * b[1] + a[1] * b[0])


def pack_kernel(own, before, after, out):
    layers, band = own.shape[1], own.shape[3]
    tiles = []
    for i in range(2):
        for k in range(layers):
            tiles.append(jnp.concatenate([before[i, k], own[i, k]], axis=1))
    for k in range(layers):
        tiles.append(jnp.concatenate([after[0, k], after[1, k]], axis=1))
    tile = jnp.stack(tiles)
    for q in range(out.shape[0]):
        out[q] = tile


def gradient_kernel(
    info, weights, probe, measured, step_l, step_r, dft_l, dft_r, mine, theirs,
    keep, send, keep_probe, send_probe, region, grown, sums, arrived, left_sem,
):
    slots, size = measured.shape[0], measured.shape[1]
    groups = region.shape[0]
    layers = groups // 3
    core = info[0]
    other = 1 - core
    copies = []
    for g in range(groups):
        copies.append(pltpu.make_async_copy(mine.at[:, g], region.at[g, :, core], arrived.at[2 * g]))
        copies.append(pltpu.make_async_copy(theirs.at[:, g], region.at[g, :, other], arrived.at[2 * g + 1]))
    for copy in copies:
        copy.start()
    grown[...] = jnp.zeros_like(grown)
    wave = (probe[0].T, probe[1].T)
    meas = [measured[p].T for p in range(slots)]
    for copy in copies:
        copy.wait()
    columns = region.shape[1] * region.shape[2] * region.shape[3]
    flat = region.reshape(groups, columns, size)
    grown_flat = grown.reshape(groups, columns, size)
    lane = lax.broadcasted_iota(jnp.int32, (size, size), 1)
    tops = [info[1 + p] for p in range(slots)]
    later = [lane < tops[p] for p in range(slots)]
    starts = [[info[1 + slots + p] + info[1 + 2 * slots + k] for k in range(layers)] for p in range(slots)]

    def window(p, k):
        at = pl.ds(starts[p][k], size)
        tail = flat[2 * layers + k, at]
        return (
            jnp.where(later[p], tail, flat[k, at]),
            jnp.where(later[p], pltpu.roll(tail, size // 2, 1), flat[layers + k, at]),
        )

    waves = [[tuple(pltpu.roll(w, tops[p], 1) for w in wave) for p in range(slots)]]
    for k in range(layers):
        leaving = [product(waves[k][p], window(p, k)) for p in range(slots)]
        if k + 1 < layers:
            waves.append(two_sided(leaving, step_l[...], step_r[...]))
        else:
            waves.append(two_sided(leaving, dft_l[...], dft_r[...]))
    back = []
    for p in range(slots):
        re, im = waves[layers][p]
        slope = (4.0 * weights[p]) * (re * re + im * im - meas[p])
        back.append((slope * re, -(slope * im)))
    for k in range(layers - 1, -1, -1):
        if k + 1 < layers:
            back = two_sided(back, step_l[...], step_r[...])
        else:
            back = two_sided(back, dft_l[...], dft_r[...])
        for p in range(slots):
            at = pl.ds(starts[p][k], size)
            re, im = product(waves[k][p], back[p])
            im = -im
            zero = jnp.zeros_like(re)
            grown_flat[k, at] += jnp.where(later[p], zero, re)
            grown_flat[layers + k, at] += jnp.where(later[p], zero, im)
            grown_flat[2 * layers + k, at] += jnp.where(later[p], re, zero) + pltpu.roll(
                jnp.where(later[p], im, zero), size // 2, 1
            )
        back = [product(window(p, k), back[p]) for p in range(slots)]
    total = []
    for i in range(2):
        total.append(
            sum(pltpu.roll(back[p][i], lax.rem(size - tops[p], size), 1) for p in range(slots))
        )
    pieces = (size // (8 * 2), 2, 8, size)
    sums[: pieces[0]] = total[0].T.reshape(pieces)
    sums[pieces[0] :] = (-total[1]).T.reshape(pieces)
    copies = [
        pltpu.make_async_copy(sums.at[:, core], keep_probe, left_sem.at[2 * groups]),
        pltpu.make_async_copy(sums.at[:, other], send_probe, left_sem.at[2 * groups + 1]),
    ]
    for g in range(groups):
        copies.append(pltpu.make_async_copy(grown.at[g, :, core], keep.at[:, g], left_sem.at[2 * g]))
        copies.append(pltpu.make_async_copy(grown.at[g, :, other], send.at[:, g], left_sem.at[2 * g + 1]))
    for copy in copies:
        copy.start()
    for copy in copies:
        copy.wait()


def spread(array, axes, count):
    return lax.all_to_all(jnp.broadcast_to(array[None], (count, *array.shape)), axes, 0, 0, tiled=True)


def local(object_slices, probe, intensities, row_offsets, column_starts, slice_shifts, counts):
    own = jnp.swapaxes(object_slices, 2, 3)
    layers, width, band = own.shape[1:]
    size = probe.shape[1]
    slots = row_offsets.shape[2]
    angles = lax.axis_size(ANGLE)
    plane = angles // 2
    scans = lax.axis_size(SCAN)
    up = [(i, i + 1) for i in range(scans - 1)]
    down = [(i + 1, i) for i in range(scans - 1)]
    swap = [(0, 1), (1, 0)]
    core = lax.axis_index("c")

    before = lax.ppermute(own, SCAN, up)
    after = lax.ppermute(own, SCAN, down)
    info = jnp.concatenate(
        [
            core.astype(jnp.int32)[None],
            row_offsets.reshape(slots),
            column_starts.reshape(slots),
            slice_shifts.reshape(layers),
        ]
    )
    weights = jnp.where(jnp.arange(slots) < counts[0, 0], 0.5 / angles, 0.0).astype(jnp.float32)
    groups = 3 * layers
    packed = pl.pallas_call(
        pack_kernel,
        out_shape=jax.ShapeDtypeStruct((plane, groups, width, 2 * band), jnp.float32),
        in_specs=[VMEM] * 3,
        out_specs=VMEM,
    )(own, before, after)
    mine = lax.all_to_all(packed, PLANE, 0, 0, tiled=True)
    theirs = lax.ppermute(mine, "c", swap)

    share = jax.ShapeDtypeStruct((plane, groups, width, size), jnp.float32)
    piece = jax.ShapeDtypeStruct((plane, 2 * size // angles, size), jnp.float32)
    keep, send, keep_probe, send_probe = pl.pallas_call(
        gradient_kernel,
        out_shape=(share, share, piece, piece),
        in_specs=[SMEM] * 2 + [VMEM] * 6 + [ANY] * 2,
        out_specs=[ANY] * 4,
        scratch_shapes=[
            pltpu.VMEM((groups, plane, 2, width, size), jnp.float32),
            pltpu.VMEM((groups, plane, 2, width, size), jnp.float32),
            pltpu.VMEM((plane, 2, 2 * size // angles, size), jnp.float32),
            pltpu.SemaphoreType.DMA((2 * groups,)),
            pltpu.SemaphoreType.DMA((2 * groups + 2,)),
        ],
        compiler_params=pltpu.CompilerParams(vmem_limit_bytes=40 * 1024 * 1024),
    )(info, weights, probe, intensities[0, 0], *[jnp.asarray(t) for t in tables(size)], mine, theirs)

    probe_part = keep_probe + lax.ppermute(send_probe, "c", swap)
    share_part = keep + lax.ppermute(send, "c", swap)
    probe_sum = lax.all_to_all(probe_part, PLANE, 0, 0, tiled=True).sum(axis=0)
    probe_sum = spread(probe_sum, SCAN, scans).sum(axis=0)
    probe_mine = spread(probe_sum, PLANE, plane)
    probe_theirs = lax.ppermute(probe_mine, "c", swap)
    probe_gradient = jnp.where(
        core == 0,
        jnp.stack([probe_mine, probe_theirs], axis=1),
        jnp.stack([probe_theirs, probe_mine], axis=1),
    ).reshape(probe.shape)

    share_sum = lax.all_to_all(share_part, PLANE, 0, 0, tiled=True).sum(axis=0)
    heads = share_sum[: 2 * layers].reshape(2, layers, width, size)
    from_after = lax.ppermute(heads[..., :band], SCAN, down)
    from_before = lax.ppermute(share_sum[2 * layers :], SCAN, up)
    object_gradient = (
        heads[..., band:] + from_after + jnp.stack([from_before[..., :band], from_before[..., band:]])
    )
    return (jnp.swapaxes(object_gradient, 2, 3), probe_gradient)


def solution(mesh):
    devices = mesh.devices.reshape(2, 8, 2, 16, 2)
    fine = Mesh(devices, ("xl", "y", "c", "z", "xh"))
    return jax.shard_map(
        local,
        mesh=fine,
        in_specs=(
            P(None, None, SCAN, ANGLE),
            P(),
            P(ANGLE, SCAN, None, None, None),
            P(ANGLE, SCAN, None),
            P(ANGLE, SCAN, None),
            P(ANGLE, None),
            P(ANGLE, SCAN),
        ),
        out_specs=(P(None, None, SCAN, ANGLE), P()),
        check_vma=False,
    )
```

time: 556 us -> 181 us (0.33)
  the two profiles are of different devices: /device:TPU:1 before, /device:TPU:8 now
where the time goes in v1:
time: 181 us; the launch traced here: 180 us
  blocking collectives  88.9 us (49%)
  waiting for transfers between devices  41.1 us (23%)
  starting transfers between devices  29.9 us (17%)
  Pallas kernels  8.68 us (5%)
  local copies, waits for them, and re-layouts  7.16 us (4%)
  other arithmetic  2.78 us (2%)
    all_to_all x1, blocking collectives, spread(): lax.all_to_all(jnp.broadcast_to(array[None], (count, *array.shape)), axes...  39.7 us
    all_to_all x1, blocking collectives, local(): mine = lax.all_to_all(packed, PLANE, 0, 0, tiled=True)  37.9 us
    all_to_all x1, waiting for transfers between devices, local(): share_sum = lax.all_to_all(share_part, PLANE, 0, 0, tiled=True).sum(axis=0)  23.6 us
    all_to_all x1, blocking collectives, local(): probe_sum = lax.all_to_all(probe_part, PLANE, 0, 0, tiled=True).sum(axis=0)  11.2 us
    pallas_call x1, Pallas kernels, local(): pl.pallas_call(gradient_kernel, out_shape=(share, share, piece, piece), i...  6.66 us
    all_to_all x1, waiting for transfers between devices, spread(): lax.all_to_all(jnp.broadcast_to(array[None], (count, *array.shape)), axes...  6.46 us
    unnamed x22, local copies, waits for them, and re-layouts  6.42 us
    ppermute x1, waiting for transfers between devices, local(): from_after = lax.ppermute(heads[..., :band], SCAN, down)  6.1 us
  transfers between devices with their start and end apart: 10, of which 7 were waited for; matrix products, arithmetic and copies ran while one was open for 2% of the time, Pallas kernels for 0%

profile of v1, /device:TPU:8, one launch (start us, length us, event | category | flops | bytes accessed | tf_op | source)
XLA Modules:
  0.0 180.0 jit_solution(5713846840578988539)
XLA Ops:
  0.6 1.3 collective-permute-start.1
  1.9 6.1 %collective-permute-start = (f32[2,3,16,64]{3,2,1,0:T(8,128)}, f32[2,3,16,64]{3,2,1,0:T(8,128)S(1)}, u32[]{:S(2)}, u32[]{:S(2)}) collective-permute-start(f32[2,3,16,64]{3,2,1,0:T(8,128)} %bitcast.26), channel_id=1, source_target_pairs={{0,1},{1,2},{2,3},{3,4},{4,5},{5,6},{6,7},{7,8},{8,9},{9,10},{10,1... | collective-permute-start | bytes 73736 | tf_op jit(solution)/shard_map/ppermute | solution.py:178
  8.3 1.7 collective-permute-done.before
  10.0 0.6 copy-done.7
  10.7 2.0 %shard_map.122 = f32[16,9,16,128]{3,2,1,0:T(8,128)} custom-call(f32[2,3,16,64]{3,2,1,0:T(8,128)} %bitcast.27, f32[2,3,16,64]{3,2,1,0:T(8,128)} %copy-done.7, f32[2,3,16,64]{3,2,1,0:T(8,128)} %copy-done.6), custom_call_target="tpu_custom_call" | custom-call | tf_op jit(solution)/shard_map/pallas_call | solution.py:190
  12.7 37.9 %all_to_all.25.mine = f32[16,9,16,128]{3,2,1,0:T(8,128)S(1)} all-to-all(f32[16,9,16,128]{3,2,1,0:T(8,128)} %shard_map.122), channel_id=1, replica_groups=mesh['xl'=2,'y'=8,'c'=2,'z'=16,'xh'=2] {'xl','y'}, dimensions={0} | all-to-all | bytes 2359296 | tf_op jit(solution)/shard_map/all_to_all | solution.py:196
  50.6 1.9 %collective-permute-start.2 = (f32[16,9,16,128]{3,2,1,0:T(8,128)S(1)}, f32[16,9,16,128]{3,2,1,0:T(8,128)S(1)}, u32[]{:S(2)}, u32[]{:S(2)}) collective-permute-start(f32[16,9,16,128]{3,2,1,0:T(8,128)S(1)} %all_to_all.25.mine), channel_id=1, source_target_pairs={{0,32},{32,0},{1,33},{33,1},{2,34},{34,2},{3,35},{35,3},{4,36},{36... | collective-permute-start | bytes 3538952 | tf_op jit(solution)/shard_map/ppermute | solution.py:197
  53.3 2.0 %collective-permute-done.2.theirs = f32[16,9,16,128]{3,2,1,0:T(8,128)S(1)} collective-permute-done((f32[16,9,16,128]{3,2,1,0:T(8,128)S(1)}, f32[16,9,16,128]{3,2,1,0:T(8,128)S(1)}, u32[]{:S(2)}, u32[]{:S(2)}) %collective-permute-start.2) | collective-permute-done | bytes 1179680 | tf_op jit(solution)/shard_map/ppermute | solution.py:197
  55.4 1.0 copy-done
  56.4 1.0 copy-done.1
  57.4 1.0 copy-done.2
  58.4 1.0 copy-done.3
  59.3 0.9 copy-done.4
  60.3 0.9 copy-done.5
  61.2 6.7 %shard_map.123 = (f32[16,9,16,128]{3,2,1,0:T(8,128)S(1)}, f32[16,9,16,128]{3,2,1,0:T(8,128)}, f32[16,8,128]{2,1,0:T(8,128)S(1)}, f32[16,8,128]{2,1,0:T(8,128)S(1)}) custom-call(s32[8]{0:T(128)S(1)} %pad_add_fusion.info, f32[2]{0:T(128)S(1)} %compare_select_fusion.weights, f32[2,128,128]{2,1,0:T(8,128)S(1)} %copy-done.4, f32[2,128,128]{2,1,0:T(8,128)S(1)} %bitcast.19, ...), custom_call_target="tpu_custom_call" | custom-call | tf_op jit(solution)/shard_map/pallas_call | solution.py:201
  67.8 2.0 %collective-permute-start.3 = (f32[16,9,16,128]{3,2,1,0:T(8,128)}, f32[16,9,16,128]{3,2,1,0:T(8,128)S(1)}, u32[]{:S(2)}, u32[]{:S(2)}) collective-permute-start(f32[16,9,16,128]{3,2,1,0:T(8,128)} %get-tuple-element.7), channel_id=1, source_target_pairs={{0,32},{32,0},{1,33},{33,1},{2,34},{34,2},{3,35},{35,3},{4,36},{36... | collective-permute-start | bytes 3538952 | tf_op jit(solution)/shard_map/ppermute | solution.py:217
  69.9 2.3 %collective-permute-start.6 = (f32[16,8,128]{2,1,0:T(8,128)S(1)}, f32[16,8,128]{2,1,0:T(8,128)S(1)}, u32[]{:S(2)}, u32[]{:S(2)}) collective-permute-start(f32[16,8,128]{2,1,0:T(8,128)S(1)} %get-tuple-element.9), channel_id=1, source_target_pairs={{0,32},{32,0},{1,33},{33,1},{2,34},{34,2},{3,35},{35,3},{4,36},{36... | collective-permute-start | bytes 196616 | tf_op jit(solution)/shard_map/ppermute | solution.py:216
  72.2 0.9 collective-permute-done.6
  73.1 11.2 %all_to_all.26 = f32[16,8,128]{2,1,0:T(8,128)S(1)} all-to-all(f32[16,8,128]{2,1,0:T(8,128)S(1)} %add.15), channel_id=1, replica_groups=mesh['xl'=2,'y'=8,'c'=2,'z'=16,'xh'=2] {'xl','y'}, dimensions={0} | all-to-all | bytes 131072 | tf_op jit(solution)/shard_map/all_to_all | solution.py:218
  84.3 39.7 %all_to_all.27 = f32[32,8,128]{2,1,0:T(8,128)S(1)} all-to-all(f32[32,8,128]{2,1,0:T(8,128)S(1)} %broadcast_in_dim.26), channel_id=1, replica_groups=mesh['xl'=2,'y'=8,'c'=2,'z'=16,'xh'=2] {'z','xh'}, dimensions={0} | all-to-all | bytes 262144 | tf_op jit(solution)/shard_map/all_to_all | solution.py:162
  124.1 0.6 broadcast_in_dim.27
  124.7 4.2 %all-to-all-start.4 = ((f32[16,8,128]{2,1,0:T(8,128)}), f32[16,8,128]{2,1,0:T(8,128)S(1)}, u32[]{:S(2)}, u32[]{:S(2)}) async-start(f32[16,8,128]{2,1,0:T(8,128)} %broadcast_in_dim.27), calls=%async_computation.4 | async-start | bytes 131072 | tf_op jit(solution)/shard_map/all_to_all | solution.py:162
  129.0 1.2 add.12
  130.1 6.5 %all-to-all-done.4 = f32[16,8,128]{2,1,0:T(8,128)S(1)} async-done(((f32[16,8,128]{2,1,0:T(8,128)}), f32[16,8,128]{2,1,0:T(8,128)S(1)}, u32[]{:S(2)}, u32[]{:S(2)}) %all-to-all-start.4) | async-done | bytes 65568 | tf_op jit(solution)/shard_map/all_to_all | solution.py:162
  136.6 4.5 %all-to-all-start.1 = ((f32[16,9,16,128]{3,2,1,0:T(8,128)}), f32[16,9,16,128]{3,2,1,0:T(8,128)S(1)}, u32[]{:S(2)}, u32[]{:S(2)}) async-start(f32[16,9,16,128]{3,2,1,0:T(8,128)} %add.12), calls=%async_computation.1 | async-start | bytes 2359296 | tf_op jit(solution)/shard_map/all_to_all | solution.py:228
  141.2 1.9 %collective-permute-start.7 = (f32[16,8,128]{2,1,0:T(8,128)S(1)}, f32[16,8,128]{2,1,0:T(8,128)S(1)}, u32[]{:S(2)}, u32[]{:S(2)}) collective-permute-start(f32[16,8,128]{2,1,0:T(8,128)S(1)} %all-to-all-done.4), channel_id=1, source_target_pairs={{0,32},{32,0},{1,33},{33,1},{2,34},{34,2},{3,35},{35,3},{4,36},{36... | collective-permute-start | bytes 196616 | tf_op jit(solution)/shard_map/ppermute | solution.py:221
  143.1 23.6 %all-to-all-done.1 = f32[16,9,16,128]{3,2,1,0:T(8,128)S(1)} async-done(((f32[16,9,16,128]{3,2,1,0:T(8,128)}), f32[16,9,16,128]{3,2,1,0:T(8,128)S(1)}, u32[]{:S(2)}, u32[]{:S(2)}) %all-to-all-start.1) | async-done | bytes 1179680 | tf_op jit(solution)/shard_map/all_to_all | solution.py:228
  166.8 4.4 %collective-permute-start.5 = (f32[3,16,128]{2,1,0:T(8,128)S(1)}, f32[3,16,128]{2,1,0:T(8,128)S(1)}, u32[]{:S(2)}, u32[]{:S(2)}) collective-permute-start(f32[3,16,128]{2,1,0:T(8,128)S(1)} %slice.27), channel_id=1, source_target_pairs={{0,1},{1,2},{2,3},{3,4},{4,5},{5,6},{6,7},{7,8},{8,9},{9,10},{10,1... | collective-permute-start | bytes 73736 | tf_op jit(solution)/shard_map/ppermute | solution.py:231
  171.2 0.7 maximum_select_fusion
  171.8 1.3 collective-permute-start.4
  173.2 6.1 %collective-permute-done.4 = f32[2,3,16,64]{3,2,1,0:T(8,128)S(1)} collective-permute-done((f32[2,3,16,64]{3,2,1,0:T(8,128)S(1)}, f32[2,3,16,64]{3,2,1,0:T(8,128)S(1)}, u32[]{:S(2)}, u32[]{:S(2)}) %collective-permute-start.4) | collective-permute-done | bytes 24608 | tf_op jit(solution)/shard_map/ppermute | solution.py:230
  179.3 0.7 fusion.1
  (29 shorter events, 0.7 us)
Async XLA Ops:
  0.6 7.7 %collective-permute-start.1 = (f32[2,3,16,64]{3,2,1,0:T(8,128)}, f32[2,3,16,64]{3,2,1,0:T(8,128)S(1)}, u32[]{:S(2)}, u32[]{:S(2)}) collective-permute-start(f32[2,3,16,64]{3,2,1,0:T(8,128)} %bitcast.25), channel_id=1, source_target_pairs={{1,0},{2,1},{3,2},{4,3},{5,4},{6,5},{7,6},{8,7},{9,8},{10,9},{11,1... | collective-permute-start | bytes 73736 | tf_op jit(solution)/shard_map/ppermute | solution.py:179
  1.9 8.1 %collective-permute-start = (f32[2,3,16,64]{3,2,1,0:T(8,128)}, f32[2,3,16,64]{3,2,1,0:T(8,128)S(1)}, u32[]{:S(2)}, u32[]{:S(2)}) collective-permute-start(f32[2,3,16,64]{3,2,1,0:T(8,128)} %bitcast.26), channel_id=1, source_target_pairs={{0,1},{1,2},{2,3},{3,4},{4,5},{5,6},{6,7},{7,8},{8,9},{9,10},{10,1... | collective-permute-start | bytes 73736 | tf_op jit(solution)/shard_map/ppermute | solution.py:178
  8.3 1.7 copy-start.6
  10.0 0.6 copy-start.7
  12.7 40.5 %copy-start.8 = (s32[1,3]{1,0:T(1,128)S(1)}, s32[1,3]{1,0:T(1,128)}, u32[]{:S(2)}) copy-start(s32[1,3]{1,0:T(1,128)} %param.16) | copy-start | bytes 40
  12.7 40.5 %copy-start.9 = (s32[1,1,2]{2,1,0:T(1,128)S(1)}, s32[1,1,2]{2,1,0:T(1,128)}, u32[]{:S(2)}) copy-start(s32[1,1,2]{2,1,0:T(1,128)} %param.15) | copy-start | bytes 28
  12.7 40.5 %copy-start.10 = (s32[1,1,2]{2,1,0:T(1,128)S(1)}, s32[1,1,2]{2,1,0:T(1,128)}, u32[]{:S(2)}) copy-start(s32[1,1,2]{2,1,0:T(1,128)} %param.14) | copy-start | bytes 28
  50.6 4.7 %collective-permute-start.2 = (f32[16,9,16,128]{3,2,1,0:T(8,128)S(1)}, f32[16,9,16,128]{3,2,1,0:T(8,128)S(1)}, u32[]{:S(2)}, u32[]{:S(2)}) collective-permute-start(f32[16,9,16,128]{3,2,1,0:T(8,128)S(1)} %all_to_all.25.mine), channel_id=1, source_target_pairs={{0,32},{32,0},{1,33},{33,1},{2,34},{34,2},{3,35},{35,3},{4,36},{36... | collective-permute-start | bytes 3538952 | tf_op jit(solution)/shard_map/ppermute | solution.py:197
  55.4 1.0 copy-start
  56.4 1.0 copy-start.1
  57.4 1.0 copy-start.2
  58.3 1.0 copy-start.3
  59.3 0.9 copy-start.4
  60.2 0.9 copy-start.5
  67.8 61.1 %collective-permute-start.3 = (f32[16,9,16,128]{3,2,1,0:T(8,128)}, f32[16,9,16,128]{3,2,1,0:T(8,128)S(1)}, u32[]{:S(2)}, u32[]{:S(2)}) collective-permute-start(f32[16,9,16,128]{3,2,1,0:T(8,128)} %get-tuple-element.7), channel_id=1, source_target_pairs={{0,32},{32,0},{1,33},{33,1},{2,34},{34,2},{3,35},{35,3},{4,36},{36... | collective-permute-start | bytes 3538952 | tf_op jit(solution)/shard_map/ppermute | solution.py:217
  69.9 3.2 %collective-permute-start.6 = (f32[16,8,128]{2,1,0:T(8,128)S(1)}, f32[16,8,128]{2,1,0:T(8,128)S(1)}, u32[]{:S(2)}, u32[]{:S(2)}) collective-permute-start(f32[16,8,128]{2,1,0:T(8,128)S(1)} %get-tuple-element.9), channel_id=1, source_target_pairs={{0,32},{32,0},{1,33},{33,1},{2,34},{34,2},{3,35},{35,3},{4,36},{36... | collective-permute-start | bytes 196616 | tf_op jit(solution)/shard_map/ppermute | solution.py:216
  124.7 11.9 %all-to-all-start.4 = ((f32[16,8,128]{2,1,0:T(8,128)}), f32[16,8,128]{2,1,0:T(8,128)S(1)}, u32[]{:S(2)}, u32[]{:S(2)}) async-start(f32[16,8,128]{2,1,0:T(8,128)} %broadcast_in_dim.27), calls=%async_computation.4 | async-start | bytes 131072 | tf_op jit(solution)/shard_map/all_to_all | solution.py:162
  136.6 30.1 %all-to-all-start.1 = ((f32[16,9,16,128]{3,2,1,0:T(8,128)}), f32[16,9,16,128]{3,2,1,0:T(8,128)S(1)}, u32[]{:S(2)}, u32[]{:S(2)}) async-start(f32[16,9,16,128]{3,2,1,0:T(8,128)} %add.12), calls=%async_computation.1 | async-start | bytes 2359296 | tf_op jit(solution)/shard_map/all_to_all | solution.py:228
  141.2 30.0 %collective-permute-start.7 = (f32[16,8,128]{2,1,0:T(8,128)S(1)}, f32[16,8,128]{2,1,0:T(8,128)S(1)}, u32[]{:S(2)}, u32[]{:S(2)}) collective-permute-start(f32[16,8,128]{2,1,0:T(8,128)S(1)} %all-to-all-done.4), channel_id=1, source_target_pairs={{0,32},{32,0},{1,33},{33,1},{2,34},{34,2},{3,35},{35,3},{4,36},{36... | collective-permute-start | bytes 196616 | tf_op jit(solution)/shard_map/ppermute | solution.py:221
  166.8 6.4 %collective-permute-start.5 = (f32[3,16,128]{2,1,0:T(8,128)S(1)}, f32[3,16,128]{2,1,0:T(8,128)S(1)}, u32[]{:S(2)}, u32[]{:S(2)}) collective-permute-start(f32[3,16,128]{2,1,0:T(8,128)S(1)} %slice.27), channel_id=1, source_target_pairs={{0,1},{1,2},{2,3},{3,4},{4,5},{5,6},{6,7},{7,8},{8,9},{9,10},{10,1... | collective-permute-start | bytes 73736 | tf_op jit(solution)/shard_map/ppermute | solution.py:231
  171.8 7.5 %collective-permute-start.4 = (f32[2,3,16,64]{3,2,1,0:T(8,128)S(1)}, f32[2,3,16,64]{3,2,1,0:T(8,128)S(1)}, u32[]{:S(2)}, u32[]{:S(2)}) collective-permute-start(f32[2,3,16,64]{3,2,1,0:T(8,128)S(1)} %bitcast.21), channel_id=1, source_target_pairs={{1,0},{2,1},{3,2},{4,3},{5,4},{6,5},{7,6},{8,7},{9,8},{10,9},{11,1... | collective-permute-start | bytes 73736 | tf_op jit(solution)/shard_map/ppermute | solution.py:230

commit v2 on v1

v2 whole, which is shorter than its diff:
```python
import jax
import jax.numpy as jnp
import numpy as np
from jax import lax
from jax.experimental import pallas as pl
from jax.experimental.pallas import tpu as pltpu
from jax.sharding import Mesh
from jax.sharding import PartitionSpec as P

PLANE = ("xl", "y")
ANGLE = ("xl", "y", "c")
SCAN = ("z", "xh")
ANY = pl.BlockSpec(memory_space=pl.ANY)
VMEM = pl.BlockSpec(memory_space=pltpu.VMEM)
SMEM = pl.BlockSpec(memory_space=pltpu.SMEM)
HBM = pl.BlockSpec(memory_space=pltpu.HBM)
SMALL = pltpu.CompilerParams(vmem_limit_bytes=8 * 1024 * 1024)


def tables(size):
    index = np.arange(size)
    centred = ((index + size // 2) % size - size // 2).astype(np.float64)
    dft = np.exp(-2j * np.pi * (np.outer(index, index) % size) / size) / np.sqrt(size)
    step = dft.conj() @ (np.exp(8j * np.pi * centred * centred / size**2)[:, None] * dft)
    whole = np.stack([np.stack([m.real, m.imag]) for m in (0.5 * (step + step.T), dft)]).astype(np.float32)
    high = whole.astype(jnp.bfloat16)
    low = (whole - high.astype(np.float32)).astype(jnp.bfloat16)
    return np.stack([high, low], axis=1)


def sides(table):
    left, right = [], []
    for part in (0, 1, 0):
        re, im = table[part, 0], table[part, 1]
        left.append(jnp.concatenate([jnp.concatenate([re, -im], axis=1), jnp.concatenate([im, re], axis=1)], axis=0))
        right.append(jnp.concatenate([jnp.concatenate([re, im], axis=1), jnp.concatenate([-im, re], axis=1)], axis=0))
    return jnp.concatenate(left, axis=1), jnp.concatenate(right, axis=0)


def parts(x, axis):
    high = x.astype(jnp.bfloat16)
    low = (x - high.astype(jnp.float32)).astype(jnp.bfloat16)
    return jnp.concatenate([high, high, low], axis=axis)


def two_sided(values, left, right):
    n = len(values)
    size = values[0][0].shape[0]
    stack = jnp.concatenate(
        [jnp.concatenate([v[i] for v in values], axis=1) for i in range(2)], axis=0
    )
    y = jnp.dot(left, parts(stack, 0), preferred_element_type=jnp.float32)
    rows = jnp.concatenate(
        [
            jnp.concatenate([y[i * size : (i + 1) * size, p * size : (p + 1) * size] for i in range(2)], axis=1)
            for p in range(n)
        ],
        axis=0,
    )
    z = jnp.dot(parts(rows, 1), right, preferred_element_type=jnp.float32)
    return [(z[p * size : (p + 1) * size, :size], z[p * size : (p + 1) * size, size:]) for p in range(n)]


def product(a, b):
    return (a[0] * b[0] - a[1] * b[1], a[0] * b[1] + a[1] * b[0])


def pack_kernel(own, out, many):
    tile = jnp.concatenate([own[0], own[1]], axis=2)
    out[...] = tile
    for q in range(many.shape[0]):
        many[q] = tile


def repeat_kernel(before, after, unused, many):
    layers = before.shape[0]
    for q in range(many.shape[0]):
        many[q, :layers] = before[...]
        many[q, layers:] = after[...]


def gradient_kernel(
    info, table, probe, measured, own_mine, own_theirs, rim_mine, rim_theirs,
    keep_near, keep_far, send_near, send_far, keep_probe, send_probe,
    region, grown, sums, table_here, probe_here, measured_here, arrived, left_sem,
):
    slots, size = measured.shape[0], measured.shape[1]
    groups = region.shape[0]
    layers = groups // 3
    half = size // 2
    rows = keep_near.shape[0]
    core = info[0]
    other = 1 - core
    near = info[1] * rows
    far = rows - near
    place = 2
    copies = []

    def fetch(source, target):
        copies.append(pltpu.make_async_copy(source, target, arrived.at[len(copies)]))

    fetch(table, table_here)
    fetch(probe, probe_here)
    fetch(measured, measured_here)
    for g in range(groups):
        mine, theirs, at = (own_mine, own_theirs, g) if g < layers else (rim_mine, rim_theirs, g - layers)
        fetch(mine.at[:, at], region.at[g, :, core])
        fetch(theirs.at[:, at], region.at[g, :, other])
    for copy in copies:
        copy.start()
    grown[...] = jnp.zeros_like(grown)
    for copy in copies:
        copy.wait()
    wave = (probe_here[0].T, probe_here[1].T)
    meas = [measured_here[p].T for p in range(slots)]
    step = sides(table_here[0])
    dft = sides(table_here[1])
    columns = region.shape[1] * region.shape[2] * region.shape[3]
    flat = region.reshape(groups, columns, size)
    grown_flat = grown.reshape(groups, columns, size)
    lane = lax.broadcasted_iota(jnp.int32, (size, size), 1)
    rim = lane < half
    folded = jnp.where(rim, lane, lane - half)
    tops = [info[place + p] for p in range(slots)]
    later = [folded < tops[p] for p in range(slots)]
    weights = [jnp.where(p < info[place + 2 * slots + layers], 4.0 * 0.5 / (4 * rows), 0.0) for p in range(slots)]
    starts = [
        [info[place + slots + p] + info[place + 2 * slots + k] for k in range(layers)] for p in range(slots)
    ]

    def window(p, k):
        at = pl.ds(starts[p][k], size)
        own = flat[k, at]
        ends = jnp.where(later[p], flat[2 * layers + k, at], flat[layers + k, at])
        return (
            jnp.where(rim, ends, pltpu.roll(own, half, 1)),
            jnp.where(rim, pltpu.roll(ends, half, 1), own),
        )

    waves = [[tuple(pltpu.roll(w, tops[p], 1) for w in wave) for p in range(slots)]]
    for k in range(layers):
        leaving = [product(waves[k][p], window(p, k)) for p in range(slots)]
        waves.append(two_sided(leaving, *(step if k + 1 < layers else dft)))
    back = []
    for p in range(slots):
        re, im = waves[layers][p]
        slope = weights[p] * (re * re + im * im - meas[p])
        back.append((slope * re, -(slope * im)))
    for k in range(layers - 1, -1, -1):
        back = two_sided(back, *(step if k + 1 < layers else dft))
        for p in range(slots):
            at = pl.ds(starts[p][k], size)
            re, im = product(waves[k][p], back[p])
            im = -im
            zero = jnp.zeros_like(re)
            ends = jnp.where(rim, re, pltpu.roll(im, half, 1))
            grown_flat[k, at] += jnp.where(rim, pltpu.roll(re, half, 1), im)
            grown_flat[layers + k, at] += jnp.where(later[p], zero, ends)
            grown_flat[2 * layers + k, at] += jnp.where(later[p], ends, zero)
        back = [product(window(p, k), back[p]) for p in range(slots)]
    total = []
    for i in range(2):
        total.append(sum(pltpu.roll(back[p][i], lax.rem(size - tops[p], size), 1) for p in range(slots)))
    pieces = (size // (8 * 2), 2, 8, size)
    sums[: pieces[0]] = total[0].T.reshape(pieces)
    sums[pieces[0] :] = (-total[1]).T.reshape(pieces)
    copies = []

    def leave(source, target):
        copies.append(pltpu.make_async_copy(source, target, left_sem.at[len(copies)]))

    leave(sums.at[:, core], keep_probe)
    leave(sums.at[:, other], send_probe)
    for g in range(groups):
        leave(grown.at[g, pl.ds(near, rows), core], keep_near.at[:, g])
        leave(grown.at[g, pl.ds(far, rows), core], keep_far.at[:, g])
        leave(grown.at[g, pl.ds(near, rows), other], send_near.at[:, g])
        leave(grown.at[g, pl.ds(far, rows), other], send_far.at[:, g])
    for copy in copies:
        copy.start()
    for copy in copies:
        copy.wait()


def scatter_sum_kernel(parts, many):
    total = parts[0]
    for q in range(1, parts.shape[0]):
        total = total + parts[q]
    for q in range(many.shape[0]):
        many[q] = total


def finish_kernel(shares, parts, own, before, after, many):
    layers = own.shape[0]
    for first, out in ((0, own), (layers, before), (2 * layers, after)):
        total = shares[0, first : first + layers]
        for q in range(1, shares.shape[0]):
            total = total + shares[q, first : first + layers]
        out[...] = total
    scatter_sum_kernel(parts, many)


def close_kernel(own, from_after, from_before, probe_mine, out, probe_out):
    probe_out[...] = probe_mine[...]
    half = own.shape[2] // 2
    total = own[...] + from_after[...] + from_before[...]
    out[0] = total[:, :, :half]
    out[1] = total[:, :, half:]


def merge_kernel(info, mine, theirs, out):
    core = info[0]
    out[:, core] = mine[...]
    out[:, 1 - core] = theirs[...]


def exchanged(array, axes):
    return lax.all_to_all(array, axes, 0, 0, tiled=True)


def local(object_slices, probe, intensities, row_offsets, column_starts, slice_shifts, counts):
    own = jnp.swapaxes(object_slices, 2, 3)
    layers, width, band = own.shape[1:]
    size = probe.shape[1]
    slots = row_offsets.shape[2]
    angles = lax.axis_size(ANGLE)
    plane = angles // 2
    rows = plane // 2
    scans = lax.axis_size(SCAN)
    up = [(i, i + 1) for i in range(scans - 1)]
    down = [(i + 1, i) for i in range(scans - 1)]
    swap = [(0, 1), (1, 0)]
    core = lax.axis_index("c")
    tile = (layers, width, 2 * band)
    groups = 3 * layers
    info = jnp.concatenate(
        [
            core.astype(jnp.int32)[None],
            lax.axis_index("xl").astype(jnp.int32)[None],
            row_offsets.reshape(slots),
            column_starts.reshape(slots),
            slice_shifts.reshape(layers),
            counts.reshape(1),
        ]
    )

    packed, packed_many = pl.pallas_call(
        pack_kernel,
        out_shape=(
            jax.ShapeDtypeStruct(tile, jnp.float32),
            jax.ShapeDtypeStruct((plane, *tile), jnp.float32),
        ),
        in_specs=[VMEM],
        out_specs=(VMEM, VMEM),
        compiler_params=SMALL,
    )(own)
    own_mine = exchanged(packed_many, PLANE)
    before = lax.ppermute(packed, SCAN, up)
    after = lax.ppermute(packed, SCAN, down)
    rim_many = pl.pallas_call(
        repeat_kernel,
        out_shape=jax.ShapeDtypeStruct((plane, 2 * layers, *tile[1:]), jnp.float32),
        in_specs=[VMEM] * 2 + [ANY],
        out_specs=VMEM,
        compiler_params=SMALL,
    )(before, after, own_mine)
    own_theirs = lax.ppermute(own_mine, "c", swap)
    rim_mine = exchanged(rim_many, PLANE)
    rim_theirs = lax.ppermute(rim_mine, "c", swap)

    share = jax.ShapeDtypeStruct((rows, groups, width, size), jnp.float32)
    piece = jax.ShapeDtypeStruct((plane, 2 * size // angles, size), jnp.float32)
    table = jnp.asarray(tables(size))
    keep_near, keep_far, send_near, send_far, keep_probe, send_probe = pl.pallas_call(
        gradient_kernel,
        out_shape=(share, share, share, share, piece, piece),
        in_specs=[SMEM] + [HBM] * 3 + [ANY] * 4,
        out_specs=[ANY] * 6,
        scratch_shapes=[
            pltpu.VMEM((groups, plane, 2, width, size), jnp.float32),
            pltpu.VMEM((groups, plane, 2, width, size), jnp.float32),
            pltpu.VMEM((plane, 2, 2 * size // angles, size), jnp.float32),
            pltpu.VMEM(table.shape, jnp.bfloat16),
            pltpu.VMEM(probe.shape, jnp.float32),
            pltpu.VMEM((slots, size, size), jnp.float32),
            pltpu.SemaphoreType.DMA((2 * groups + 3,)),
            pltpu.SemaphoreType.DMA((4 * groups + 2,)),
        ],
        compiler_params=pltpu.CompilerParams(vmem_limit_bytes=32 * 1024 * 1024),
    )(info, table, probe, intensities[0, 0], own_mine, own_theirs, rim_mine, rim_theirs)

    probe_part = keep_probe + lax.ppermute(send_probe, "c", swap)
    probe_part, send_far, send_near = lax.optimization_barrier((probe_part, send_far, send_near))
    bit = probe_part.shape[1:]
    probe_many = pl.pallas_call(
        scatter_sum_kernel,
        out_shape=jax.ShapeDtypeStruct((scans, *bit), jnp.float32),
        in_specs=[VMEM],
        out_specs=VMEM,
        compiler_params=SMALL,
    )(exchanged(probe_part, PLANE))
    probe_many = exchanged(probe_many, SCAN)

    part_far = keep_far + lax.ppermute(send_far, "c", swap)
    part_near = keep_near + lax.ppermute(send_near, "c", swap)
    part = part_near + lax.ppermute(part_far, "xl", swap)
    tile_out = jax.ShapeDtypeStruct(tile, jnp.float32)
    own_sum, to_before, to_after, probe_many = pl.pallas_call(
        finish_kernel,
        out_shape=(tile_out, tile_out, tile_out, jax.ShapeDtypeStruct((plane, *bit), jnp.float32)),
        in_specs=[VMEM] * 2,
        out_specs=[VMEM] * 4,
        compiler_params=SMALL,
    )(exchanged(part, "y"), probe_many)

    probe_mine = exchanged(probe_many, PLANE)
    from_after = lax.ppermute(to_before, SCAN, down)
    from_before = lax.ppermute(to_after, SCAN, up)
    object_gradient, probe_mine = pl.pallas_call(
        close_kernel,
        out_shape=(
            jax.ShapeDtypeStruct(own.shape, jnp.float32),
            jax.ShapeDtypeStruct(probe_mine.shape, jnp.float32),
        ),
        in_specs=[VMEM] * 4,
        out_specs=(VMEM, VMEM),
        compiler_params=SMALL,
    )(own_sum, from_after, from_before, probe_mine)
    probe_theirs = lax.ppermute(probe_mine, "c", swap)
    probe_gradient = pl.pallas_call(
        merge_kernel,
        out_shape=jax.ShapeDtypeStruct((plane, 2, *bit), jnp.float32),
        in_specs=[SMEM, VMEM, VMEM],
        out_specs=VMEM,
        compiler_params=SMALL,
    )(info, probe_mine, probe_theirs).reshape(probe.shape)
    return (jnp.swapaxes(object_gradient, 2, 3), probe_gradient)


def solution(mesh):
    devices = mesh.devices.reshape(2, 8, 2, 16, 2)
    fine = Mesh(devices, ("xl", "y", "c", "z", "xh"))
    return jax.shard_map(
        local,
        mesh=fine,
        in_specs=(
            P(None, None, SCAN, ANGLE),
            P(),
            P(ANGLE, SCAN, None, None, None),
            P(ANGLE, SCAN, None),
            P(ANGLE, SCAN, None),
            P(ANGLE, None),
            P(ANGLE, SCAN),
        ),
        out_specs=(P(None, None, SCAN, ANGLE), P()),
        check_vma=False,
    )
```

time: 181 us -> 170 us (0.939)
  the two profiles are of different devices: /device:TPU:8 before, /device:TPU:1 now
where the time goes in v2:
time: 170 us; the launch traced here: 167 us
  starting transfers between devices  80.4 us (47%)
  blocking collectives  51.3 us (30%)
  waiting for transfers between devices  20.1 us (12%)
  Pallas kernels  11.3 us (7%)
    all_to_all x3, blocking collectives, exchanged(): return lax.all_to_all(array, axes, 0, 0, tiled=True)  51.3 us
    all_to_all x3, starting transfers between devices, exchanged(): return lax.all_to_all(array, axes, 0, 0, tiled=True)  33.8 us
    all_to_all x3, waiting for transfers between devices, exchanged(): return lax.all_to_all(array, axes, 0, 0, tiled=True)  16.2 us
    ppermute x1, starting transfers between devices, local(): rim_theirs = lax.ppermute(rim_mine, 'c', swap)  13.7 us
    ppermute x1, starting transfers between devices, local(): probe_theirs = lax.ppermute(probe_mine, 'c', swap)  7.99 us
    pallas_call x1, Pallas kernels, local(): pl.pallas_call(gradient_kernel, out_shape=(share, share, share, share, pi...  7.2 us
    ppermute x1, starting transfers between devices, local(): before = lax.ppermute(packed, SCAN, up)  5.49 us
    ppermute x1, starting transfers between devices, local(): from_before = lax.ppermute(to_after, SCAN, up)  5.49 us
  transfers between devices with their start and end apart: 14, of which 7 were waited for; matrix products, arithmetic and copies ran while one was open for 0% of the time, Pallas kernels for 0%

profile of v2, /device:TPU:1, one launch (start us, length us, event | category | flops | bytes accessed | tf_op | source)
XLA Modules:
  0.0 166.6 jit_solution(15782244649483978495)
XLA Ops:
  0.6 0.8 copy-done.3
  1.4 0.8 shard_map.95
  2.3 8.7 %all-to-all-start = ((f32[16,3,16,128]{3,2,1,0:T(8,128)}), f32[16,3,16,128]{3,2,1,0:T(8,128)S(1)}, u32[]{:S(2)}, u32[]{:S(2)}) async-start(f32[16,3,16,128]{3,2,1,0:T(8,128)} %get-tuple-element.19), calls=%async_computation | async-start | bytes 786432 | tf_op jit(solution)/shard_map/all_to_all | solution.py:218
  11.0 1.3 collective-permute-start.2
  12.3 5.5 %collective-permute-start.1 = (f32[3,16,128]{2,1,0:T(8,128)S(1)}, f32[3,16,128]{2,1,0:T(8,128)S(1)}, u32[]{:S(2)}, u32[]{:S(2)}) collective-permute-start(f32[3,16,128]{2,1,0:T(8,128)S(1)} %get-tuple-element.20), channel_id=1, source_target_pairs={{0,1},{1,2},{2,3},{3,4},{4,5},{5,6},{6,7},{7,8},{8,9},{9,10},{10,1... | collective-permute-start | bytes 73736 | tf_op jit(solution)/shard_map/ppermute | solution.py:258
  17.8 0.9 collective-permute-done.1.before
  18.7 1.5 all-to-all-done.unused.own_mine
  20.3 19.0 %all_to_all.30.rim_mine = f32[16,6,16,128]{3,2,1,0:T(8,128)S(1)} all-to-all(f32[16,6,16,128]{3,2,1,0:T(8,128)S(1)} %shard_map.96), channel_id=1, replica_groups=mesh['xl'=2,'y'=8,'c'=2,'z'=16,'xh'=2] {'xl','y'}, dimensions={0} | all-to-all | bytes 1572864 | tf_op jit(solution)/shard_map/all_to_all | solution.py:218
  39.4 13.7 %collective-permute-start.3 = (f32[16,6,16,128]{3,2,1,0:T(8,128)S(1)}, f32[16,6,16,128]{3,2,1,0:T(8,128)S(1)}, u32[]{:S(2)}, u32[]{:S(2)}) collective-permute-start(f32[16,6,16,128]{3,2,1,0:T(8,128)S(1)} %all_to_all.30.rim_mine), channel_id=1, source_target_pairs={{0,32},{32,0},{1,33},{33,1},{2,34},{34,2},{3,35},{35,3},{4,36},{36... | collective-permute-start | bytes 2359304 | tf_op jit(solution)/shard_map/ppermute | solution.py:269
  53.1 1.9 %collective-permute-start = (f32[16,3,16,128]{3,2,1,0:T(8,128)S(1)}, f32[16,3,16,128]{3,2,1,0:T(8,128)S(1)}, u32[]{:S(2)}, u32[]{:S(2)}) collective-permute-start(f32[16,3,16,128]{3,2,1,0:T(8,128)S(1)} %all-to-all-done.unused.own_mine), channel_id=1, source_target_pairs={{0,32},{32,0},{1,33},{33,1},{2,34},{34,2},{3,35},{35,3},{4,36},{36... | collective-permute-start | bytes 1179656 | tf_op jit(solution)/shard_map/ppermute | solution.py:267
  55.7 0.6 copy-done.4
  56.4 0.3 collective-permute-done.own_theirs
  56.7 7.2 %shard_map.97 = (f32[8,9,16,128]{3,2,1,0:T(8,128)S(1)}, f32[8,9,16,128]{3,2,1,0:T(8,128)S(1)}, f32[8,9,16,128]{3,2,1,0:T(8,128)}, f32[8,9,16,128]{3,2,1,0:T(8,12...) custom-call(s32[10]{0:T(128)S(1)} %concatenate.3.info, bf16[2,2,2,128,128]{4,3,2,1,0:T(8,128)(2,1)S(1)} %copy-done, ...), custom_call_target="tpu_custom_call" | custom-call | tf_op jit(solution)/shard_map/pallas_call | solution.py:274
  63.9 2.1 %collective-permute-start.4 = (f32[16,8,128]{2,1,0:T(8,128)S(1)}, f32[16,8,128]{2,1,0:T(8,128)S(1)}, u32[]{:S(2)}, u32[]{:S(2)}) collective-permute-start(f32[16,8,128]{2,1,0:T(8,128)S(1)} %get-tuple-element.23), channel_id=1, source_target_pairs={{0,32},{32,0},{1,33},{33,1},{2,34},{34,2},{3,35},{35,3},{4,36},{36... | collective-permute-start | bytes 196616 | tf_op jit(solution)/shard_map/ppermute | solution.py:292
  66.1 1.0 collective-permute-done.4
  67.1 2.1 %collective-permute-start.6 = (f32[8,9,16,128]{3,2,1,0:T(8,128)S(1)}, f32[8,9,16,128]{3,2,1,0:T(8,128)S(1)}, u32[]{:S(2)}, u32[]{:S(2)}) collective-permute-start(f32[8,9,16,128]{3,2,1,0:T(8,128)S(1)} %get-tuple-element.28), channel_id=1, source_target_pairs={{0,32},{32,0},{1,33},{33,1},{2,34},{34,2},{3,35},{35,3},{4,36},{36... | collective-permute-start | bytes 1769480 | tf_op jit(solution)/shard_map/ppermute | solution.py:304
  69.3 2.2 %collective-permute-start.5 = (f32[8,9,16,128]{3,2,1,0:T(8,128)}, f32[8,9,16,128]{3,2,1,0:T(8,128)S(1)}, u32[]{:S(2)}, u32[]{:S(2)}) collective-permute-start(f32[8,9,16,128]{3,2,1,0:T(8,128)} %get-tuple-element.26), channel_id=1, source_target_pairs={{0,32},{32,0},{1,33},{33,1},{2,34},{34,2},{3,35},{35,3},{4,36},{36... | collective-permute-start | bytes 1769480 | tf_op jit(solution)/shard_map/ppermute | solution.py:305
  71.5 2.9 %collective-permute-start.7 = (f32[8,9,16,128]{3,2,1,0:T(8,128)S(1)}, f32[8,9,16,128]{3,2,1,0:T(8,128)S(1)}, u32[]{:S(2)}, u32[]{:S(2)}) collective-permute-start(f32[8,9,16,128]{3,2,1,0:T(8,128)S(1)} %add.14), channel_id=1, source_target_pairs={{0,512},{512,0},{1,513},{513,1},{2,514},{514,2},{3,515},{515,3},{4... | collective-permute-start | bytes 1769480 | tf_op jit(solution)/shard_map/ppermute | solution.py:306
  74.5 14.4 %all_to_all.31.parts = f32[16,8,128]{2,1,0:T(8,128)S(1)} all-to-all(f32[16,8,128]{2,1,0:T(8,128)S(1)} %add.12), channel_id=1, replica_groups=mesh['xl'=2,'y'=8,'c'=2,'z'=16,'xh'=2] {'xl','y'}, dimensions={0} | all-to-all | bytes 131072 | tf_op jit(solution)/shard_map/all_to_all | solution.py:218
  88.8 0.7 shard_map.98
  89.5 21.0 %all-to-all-start.4 = ((f32[32,8,128]{2,1,0:T(8,128)}), f32[32,8,128]{2,1,0:T(8,128)S(1)}, u32[]{:S(2)}, u32[]{:S(2)}) async-start(f32[32,8,128]{2,1,0:T(8,128)} %shard_map.98), calls=%async_computation.4 | async-start | bytes 262144 | tf_op jit(solution)/shard_map/all_to_all | solution.py:218
  110.6 14.6 %all-to-all-done.4.parts = f32[32,8,128]{2,1,0:T(8,128)S(1)} async-done(((f32[32,8,128]{2,1,0:T(8,128)}), f32[32,8,128]{2,1,0:T(8,128)S(1)}, u32[]{:S(2)}, u32[]{:S(2)}) %all-to-all-start.4) | async-done | bytes 131104 | tf_op jit(solution)/shard_map/all_to_all | solution.py:218
  125.2 17.9 %all_to_all.32.shares = f32[8,9,16,128]{3,2,1,0:T(8,128)S(1)} all-to-all(f32[8,9,16,128]{3,2,1,0:T(8,128)S(1)} %add_add_fusion), channel_id=1, replica_groups=mesh['xl'=2,'y'=8,'c'=2,'z'=16,'xh'=2] {'y'}, dimensions={0} | all-to-all | bytes 1179648 | tf_op jit(solution)/shard_map/all_to_all | solution.py:218
  143.2 0.7 shard_map.99
  143.8 4.2 %all-to-all-start.5 = ((f32[16,8,128]{2,1,0:T(8,128)}), f32[16,8,128]{2,1,0:T(8,128)S(1)}, u32[]{:S(2)}, u32[]{:S(2)}) async-start(f32[16,8,128]{2,1,0:T(8,128)} %get-tuple-element.33), calls=%async_computation.5 | async-start | bytes 131072 | tf_op jit(solution)/shard_map/all_to_all | solution.py:218
  148.0 1.3 collective-permute-start.8
  149.3 5.5 %collective-permute-start.9 = (f32[3,16,128]{2,1,0:T(8,128)S(1)}, f32[3,16,128]{2,1,0:T(8,128)S(1)}, u32[]{:S(2)}, u32[]{:S(2)}) collective-permute-start(f32[3,16,128]{2,1,0:T(8,128)S(1)} %get-tuple-element.32), channel_id=1, source_target_pairs={{0,1},{1,2},{2,3},{3,4},{4,5},{5,6},{6,7},{7,8},{8,9},{9,10},{10,1... | collective-permute-start | bytes 73736 | tf_op jit(solution)/shard_map/ppermute | solution.py:318
  154.9 0.9 collective-permute-done.9.from_before
  155.8 0.7 shard_map.100
  156.5 8.0 %collective-permute-start.10 = (f32[16,8,128]{2,1,0:T(8,128)S(1)}, f32[16,8,128]{2,1,0:T(8,128)S(1)}, u32[]{:S(2)}, u32[]{:S(2)}) collective-permute-start(f32[16,8,128]{2,1,0:T(8,128)S(1)} %get-tuple-element.35.mine), channel_id=1, source_target_pairs={{0,32},{32,0},{1,33},{33,1},{2,34},{34,2},{3,35},{35,3},{4,36},{36... | collective-permute-start | bytes 196616 | tf_op jit(solution)/shard_map/ppermute | solution.py:329
  164.5 0.9 collective-permute-done.10.theirs
  165.4 1.2 shard_map.101
  (24 shorter events, 0.4 us)
Async XLA Ops:
  0.6 0.8 copy-start.3
  2.3 18.0 %all-to-all-start = ((f32[16,3,16,128]{3,2,1,0:T(8,128)}), f32[16,3,16,128]{3,2,1,0:T(8,128)S(1)}, u32[]{:S(2)}, u32[]{:S(2)}) async-start(f32[16,3,16,128]{3,2,1,0:T(8,128)} %get-tuple-element.19), calls=%async_computation | async-start | bytes 786432 | tf_op jit(solution)/shard_map/all_to_all | solution.py:218
  11.0 6.8 %collective-permute-start.2 = (f32[3,16,128]{2,1,0:T(8,128)S(1)}, f32[3,16,128]{2,1,0:T(8,128)S(1)}, u32[]{:S(2)}, u32[]{:S(2)}) collective-permute-start(f32[3,16,128]{2,1,0:T(8,128)S(1)} %get-tuple-element.20), channel_id=1, source_target_pairs={{1,0},{2,1},{3,2},{4,3},{5,4},{6,5},{7,6},{8,7},{9,8},{10,9},{11,1... | collective-permute-start | bytes 73736 | tf_op jit(solution)/shard_map/ppermute | solution.py:259
  12.3 6.4 %collective-permute-start.1 = (f32[3,16,128]{2,1,0:T(8,128)S(1)}, f32[3,16,128]{2,1,0:T(8,128)S(1)}, u32[]{:S(2)}, u32[]{:S(2)}) collective-permute-start(f32[3,16,128]{2,1,0:T(8,128)S(1)} %get-tuple-element.20), channel_id=1, source_target_pairs={{0,1},{1,2},{2,3},{3,4},{4,5},{5,6},{6,7},{7,8},{8,9},{9,10},{10,1... | collective-permute-start | bytes 73736 | tf_op jit(solution)/shard_map/ppermute | solution.py:258
  20.3 36.4 %copy-start = (bf16[2,2,2,128,128]{4,3,2,1,0:T(8,128)(2,1)S(1)}, bf16[2,2,2,128,128]{4,3,2,1,0:T(8,128)(2,1)}, u32[]{:S(2)}) copy-start(bf16[2,2,2,128,128]{4,3,2,1,0:T(8,128)(2,1)} %constant.12.clone.table) | copy-start | bytes 786436
  20.3 36.4 %copy-start.1 = (f32[2,128,128]{2,1,0:T(8,128)S(1)}, f32[2,128,128]{2,1,0:T(8,128)}, u32[]{:S(2)}) copy-start(f32[2,128,128]{2,1,0:T(8,128)} %probe.1) | copy-start | bytes 393220
  20.3 36.4 %copy-start.2 = (f32[1,1,2,128,128]{4,3,2,1,0:T(8,128)S(1)}, f32[1,1,2,128,128]{4,3,2,1,0:T(8,128)}, u32[]{:S(2)}) copy-start(f32[1,1,2,128,128]{4,3,2,1,0:T(8,128)} %param.10) | copy-start | bytes 393220
  39.4 17.3 %collective-permute-start.3 = (f32[16,6,16,128]{3,2,1,0:T(8,128)S(1)}, f32[16,6,16,128]{3,2,1,0:T(8,128)S(1)}, u32[]{:S(2)}, u32[]{:S(2)}) collective-permute-start(f32[16,6,16,128]{3,2,1,0:T(8,128)S(1)} %all_to_all.30.rim_mine), channel_id=1, source_target_pairs={{0,32},{32,0},{1,33},{33,1},{2,34},{34,2},{3,35},{35,3},{4,36},{36... | collective-permute-start | bytes 2359304 | tf_op jit(solution)/shard_map/ppermute | solution.py:269
  53.1 3.6 %collective-permute-start = (f32[16,3,16,128]{3,2,1,0:T(8,128)S(1)}, f32[16,3,16,128]{3,2,1,0:T(8,128)S(1)}, u32[]{:S(2)}, u32[]{:S(2)}) collective-permute-start(f32[16,3,16,128]{3,2,1,0:T(8,128)S(1)} %all-to-all-done.unused.own_mine), channel_id=1, source_target_pairs={{0,32},{32,0},{1,33},{33,1},{2,34},{34,2},{3,35},{35,3},{4,36},{36... | collective-permute-start | bytes 1179656 | tf_op jit(solution)/shard_map/ppermute | solution.py:267
  55.7 0.7 copy-start.4
  55.7 0.7 copy-start.5
  55.7 0.7 copy-start.6
  63.9 3.1 %collective-permute-start.4 = (f32[16,8,128]{2,1,0:T(8,128)S(1)}, f32[16,8,128]{2,1,0:T(8,128)S(1)}, u32[]{:S(2)}, u32[]{:S(2)}) collective-permute-start(f32[16,8,128]{2,1,0:T(8,128)S(1)} %get-tuple-element.23), channel_id=1, source_target_pairs={{0,32},{32,0},{1,33},{33,1},{2,34},{34,2},{3,35},{35,3},{4,36},{36... | collective-permute-start | bytes 196616 | tf_op jit(solution)/shard_map/ppermute | solution.py:292
  67.1 4.3 %collective-permute-start.6 = (f32[8,9,16,128]{3,2,1,0:T(8,128)S(1)}, f32[8,9,16,128]{3,2,1,0:T(8,128)S(1)}, u32[]{:S(2)}, u32[]{:S(2)}) collective-permute-start(f32[8,9,16,128]{3,2,1,0:T(8,128)S(1)} %get-tuple-element.28), channel_id=1, source_target_pairs={{0,32},{32,0},{1,33},{33,1},{2,34},{34,2},{3,35},{35,3},{4,36},{36... | collective-permute-start | bytes 1769480 | tf_op jit(solution)/shard_map/ppermute | solution.py:304
  69.3 41.2 %collective-permute-start.5 = (f32[8,9,16,128]{3,2,1,0:T(8,128)}, f32[8,9,16,128]{3,2,1,0:T(8,128)S(1)}, u32[]{:S(2)}, u32[]{:S(2)}) collective-permute-start(f32[8,9,16,128]{3,2,1,0:T(8,128)} %get-tuple-element.26), channel_id=1, source_target_pairs={{0,32},{32,0},{1,33},{33,1},{2,34},{34,2},{3,35},{35,3},{4,36},{36... | collective-permute-start | bytes 1769480 | tf_op jit(solution)/shard_map/ppermute | solution.py:305
  71.5 39.0 %collective-permute-start.7 = (f32[8,9,16,128]{3,2,1,0:T(8,128)S(1)}, f32[8,9,16,128]{3,2,1,0:T(8,128)S(1)}, u32[]{:S(2)}, u32[]{:S(2)}) collective-permute-start(f32[8,9,16,128]{3,2,1,0:T(8,128)S(1)} %add.14), channel_id=1, source_target_pairs={{0,512},{512,0},{1,513},{513,1},{2,514},{514,2},{3,515},{515,3},{4... | collective-permute-start | bytes 1769480 | tf_op jit(solution)/shard_map/ppermute | solution.py:306
  89.5 35.7 %all-to-all-start.4 = ((f32[32,8,128]{2,1,0:T(8,128)}), f32[32,8,128]{2,1,0:T(8,128)S(1)}, u32[]{:S(2)}, u32[]{:S(2)}) async-start(f32[32,8,128]{2,1,0:T(8,128)} %shard_map.98), calls=%async_computation.4 | async-start | bytes 262144 | tf_op jit(solution)/shard_map/all_to_all | solution.py:218
  143.8 11.9 %all-to-all-start.5 = ((f32[16,8,128]{2,1,0:T(8,128)}), f32[16,8,128]{2,1,0:T(8,128)S(1)}, u32[]{:S(2)}, u32[]{:S(2)}) async-start(f32[16,8,128]{2,1,0:T(8,128)} %get-tuple-element.33), calls=%async_computation.5 | async-start | bytes 131072 | tf_op jit(solution)/shard_map/all_to_all | solution.py:218
  148.0 6.8 %collective-permute-start.8 = (f32[3,16,128]{2,1,0:T(8,128)S(1)}, f32[3,16,128]{2,1,0:T(8,128)S(1)}, u32[]{:S(2)}, u32[]{:S(2)}) collective-permute-start(f32[3,16,128]{2,1,0:T(8,128)S(1)} %get-tuple-element.31), channel_id=1, source_target_pairs={{1,0},{2,1},{3,2},{4,3},{5,4},{6,5},{7,6},{8,7},{9,8},{10,9},{11,1... | collective-permute-start | bytes 73736 | tf_op jit(solution)/shard_map/ppermute | solution.py:317
  149.3 6.4 %collective-permute-start.9 = (f32[3,16,128]{2,1,0:T(8,128)S(1)}, f32[3,16,128]{2,1,0:T(8,128)S(1)}, u32[]{:S(2)}, u32[]{:S(2)}) collective-permute-start(f32[3,16,128]{2,1,0:T(8,128)S(1)} %get-tuple-element.32), channel_id=1, source_target_pairs={{0,1},{1,2},{2,3},{3,4},{4,5},{5,6},{6,7},{7,8},{8,9},{9,10},{10,1... | collective-permute-start | bytes 73736 | tf_op jit(solution)/shard_map/ppermute | solution.py:318
  156.5 8.9 %collective-permute-start.10 = (f32[16,8,128]{2,1,0:T(8,128)S(1)}, f32[16,8,128]{2,1,0:T(8,128)S(1)}, u32[]{:S(2)}, u32[]{:S(2)}) collective-permute-start(f32[16,8,128]{2,1,0:T(8,128)S(1)} %get-tuple-element.35.mine), channel_id=1, source_target_pairs={{0,32},{32,0},{1,33},{33,1},{2,34},{34,2},{3,35},{35,3},{4,36},{36... | collective-permute-start | bytes 196616 | tf_op jit(solution)/shard_map/ppermute | solution.py:329

commit v3 on v2

--- a/solution.py
+++ b/solution.py
@@ -10,10 +10,12 @@
 PLANE = ("xl", "y")
 ANGLE = ("xl", "y", "c")
 SCAN = ("z", "xh")
+ROW = ("xl", "c", "xh")
 ANY = pl.BlockSpec(memory_space=pl.ANY)
 VMEM = pl.BlockSpec(memory_space=pltpu.VMEM)
 SMEM = pl.BlockSpec(memory_space=pltpu.SMEM)
 HBM = pl.BlockSpec(memory_space=pltpu.HBM)
+URGENT = pl.CostEstimate(flops=50_000_000_000, bytes_accessed=1_000_000, transcendentals=0)
 SMALL = pltpu.CompilerParams(vmem_limit_bytes=8 * 1024 * 1024)
 
 
@@ -72,16 +74,19 @@
         many[q] = tile
 
 
-def repeat_kernel(before, after, unused, many):
-    layers = before.shape[0]
+def repeat_kernel(info, paired, crossed, unused, many):
+    layers = paired.shape[0]
+    odd = info[0] == 1
+    before = jnp.where(odd, paired[...], crossed[...])
+    after = jnp.where(odd, crossed[...], paired[...])
     for q in range(many.shape[0]):
-        many[q, :layers] = before[...]
-        many[q, layers:] = after[...]
+        many[q, :layers] = before
+        many[q, layers:] = after
 
 
 def gradient_kernel(
     info, table, probe, measured, own_mine, own_theirs, rim_mine, rim_theirs,
-    keep_near, keep_far, send_near, send_far, keep_probe, send_probe,
+    keep_near, keep_far, send_near, send_far, probe_sums,
     region, grown, sums, table_here, probe_here, measured_here, arrived, left_sem,
 ):
     slots, size = measured.shape[0], measured.shape[1]
@@ -161,16 +166,15 @@
     total = []
     for i in range(2):
         total.append(sum(pltpu.roll(back[p][i], lax.rem(size - tops[p], size), 1) for p in range(slots)))
-    pieces = (size // (8 * 2), 2, 8, size)
-    sums[: pieces[0]] = total[0].T.reshape(pieces)
-    sums[pieces[0] :] = (-total[1]).T.reshape(pieces)
+    pieces = sums.shape[0] // 2
+    sums[:pieces] = total[0].T.reshape(pieces, *sums.shape[1:])
+    sums[pieces:] = (-total[1]).T.reshape(pieces, *sums.shape[1:])
     copies = []
 
     def leave(source, target):
         copies.append(pltpu.make_async_copy(source, target, left_sem.at[len(copies)]))
 
-    leave(sums.at[:, core], keep_probe)
-    leave(sums.at[:, other], send_probe)
+    leave(sums, probe_sums)
     for g in range(groups):
         leave(grown.at[g, pl.ds(near, rows), core], keep_near.at[:, g])
         leave(grown.at[g, pl.ds(far, rows), core], keep_far.at[:, g])
@@ -182,36 +186,46 @@
         copy.wait()
 
 
-def scatter_sum_kernel(parts, many):
-    total = parts[0]
+def summed(parts, first, last):
+    total = parts[0, first:last]
     for q in range(1, parts.shape[0]):
-        total = total + parts[q]
+        total = total + parts[q, first:last]
+    return total
+
+
+def probe_kernel(parts, many):
+    total = summed(parts, 0, parts.shape[1])
     for q in range(many.shape[0]):
         many[q] = total
 
 
-def finish_kernel(shares, parts, own, before, after, many):
-    layers = own.shape[0]
-    for first, out in ((0, own), (layers, before), (2 * layers, after)):
-        total = shares[0, first : first + layers]
-        for q in range(1, shares.shape[0]):
-            total = total + shares[q, first : first + layers]
-        out[...] = total
-    scatter_sum_kernel(parts, many)
-
-
-def close_kernel(own, from_after, from_before, probe_mine, out, probe_out):
-    probe_out[...] = probe_mine[...]
-    half = own.shape[2] // 2
-    total = own[...] + from_after[...] + from_before[...]
-    out[0] = total[:, :, :half]
-    out[1] = total[:, :, half:]
-
-
-def merge_kernel(info, mine, theirs, out):
-    core = info[0]
-    out[:, core] = mine[...]
-    out[:, 1 - core] = theirs[...]
+def share_kernel(info, kept, swapped, crossed, own, to_paired, to_crossed):
+    layers = own.shape[1]
+    odd = info[0] == 1
+    for q in range(own.shape[0]):
+        total = kept[q] + swapped[q] + crossed[q]
+        before, after = total[layers : 2 * layers], total[2 * layers :]
+        own[q] = total[:layers]
+        to_paired[q] = jnp.where(odd, before, after)
+        to_crossed[q] = jnp.where(odd, after, before)
+
+
+def join_kernel(own, from_paired, from_crossed, parts, out):
+    layers = own.shape[1]
+    total = summed(parts, 0, parts.shape[1])
+    total = total.reshape(out.shape[1] - layers, *out.shape[2:])
+    for q in range(out.shape[0]):
+        out[q, :layers] = own[q] + from_paired[q] + from_crossed[q]
+        out[q, layers:] = total
+
+
+def finish_kernel(shares, object_out, probe_out):
+    layers, half = object_out.shape[1], object_out.shape[3]
+    total = summed(shares, 0, layers)
+    object_out[0] = total[:, :, :half]
+    object_out[1] = total[:, :, half:]
+    for q in range(shares.shape[0]):
+        probe_out[q] = shares[q, layers:].reshape(probe_out.shape[1:])
 
 
 def exchanged(array, axes):
@@ -227,8 +241,9 @@
     plane = angles // 2
     rows = plane // 2
     scans = lax.axis_size(SCAN)
-    up = [(i, i + 1) for i in range(scans - 1)]
-    down = [(i + 1, i) for i in range(scans - 1)]
+    pairs = [(i, i ^ 1) for i in range(scans)]
+    others = [(i, i + 1 if i % 2 else i - 1) for i in range(1, scans - 1)]
+    odd = lax.axis_index("xh").astype(jnp.int32)[None]
     swap = [(0, 1), (1, 0)]
     core = lax.axis_index("c")
     tile = (layers, width, 2 * band)
@@ -255,86 +270,84 @@
         compiler_params=SMALL,
     )(own)
     own_mine = exchanged(packed_many, PLANE)
-    before = lax.ppermute(packed, SCAN, up)
-    after = lax.ppermute(packed, SCAN, down)
+    paired = lax.ppermute(packed, SCAN, pairs)
+    crossed = lax.ppermute(packed, SCAN, others)
     rim_many = pl.pallas_call(
         repeat_kernel,
         out_shape=jax.ShapeDtypeStruct((plane, 2 * layers, *tile[1:]), jnp.float32),
-        in_specs=[VMEM] * 2 + [ANY],
+        in_specs=[SMEM] + [VMEM] * 2 + [ANY],
         out_specs=VMEM,
         compiler_params=SMALL,
-    )(before, after, own_mine)
+    )(odd, paired, crossed, own_mine)
     own_theirs = lax.ppermute(own_mine, "c", swap)
     rim_mine = exchanged(rim_many, PLANE)
     rim_theirs = lax.ppermute(rim_mine, "c", swap)
 
     share = jax.ShapeDtypeStruct((rows, groups, width, size), jnp.float32)
-    piece = jax.ShapeDtypeStruct((plane, 2 * size // angles, size), jnp.float32)
+    depth = lax.axis_size("z")
+    piece = jax.ShapeDtypeStruct((rows, 2 * size // rows, size), jnp.float32)
     table = jnp.asarray(tables(size))
-    keep_near, keep_far, send_near, send_far, keep_probe, send_probe = pl.pallas_call(
+    keep_near, keep_far, send_near, send_far, probe_sums = pl.pallas_call(
         gradient_kernel,
-        out_shape=(share, share, share, share, piece, piece),
+        out_shape=(share, share, share, share, piece),
         in_specs=[SMEM] + [HBM] * 3 + [ANY] * 4,
-        out_specs=[ANY] * 6,
+        out_specs=[HBM] * 5,
         scratch_shapes=[
             pltpu.VMEM((groups, plane, 2, width, size), jnp.float32),
             pltpu.VMEM((groups, plane, 2, width, size), jnp.float32),
-            pltpu.VMEM((plane, 2, 2 * size // angles, size), jnp.float32),
+            pltpu.VMEM(piece.shape, jnp.float32),
             pltpu.VMEM(table.shape, jnp.bfloat16),
             pltpu.VMEM(probe.shape, jnp.float32),
             pltpu.VMEM((slots, size, size), jnp.float32),
             pltpu.SemaphoreType.DMA((2 * groups + 3,)),
-            pltpu.SemaphoreType.DMA((4 * groups + 2,)),
+            pltpu.SemaphoreType.DMA((4 * groups + 1,)),
         ],
-        compiler_params=pltpu.CompilerParams(vmem_limit_bytes=32 * 1024 * 1024),
+        compiler_params=pltpu.CompilerParams(vmem_limit_bytes=52 * 1024 * 1024),
     )(info, table, probe, intensities[0, 0], own_mine, own_theirs, rim_mine, rim_theirs)
 
-    probe_part = keep_probe + lax.ppermute(send_probe, "c", swap)
-    probe_part, send_far, send_near = lax.optimization_barrier((probe_part, send_far, send_near))
-    bit = probe_part.shape[1:]
-    probe_many = pl.pallas_call(
-        scatter_sum_kernel,
-        out_shape=jax.ShapeDtypeStruct((scans, *bit), jnp.float32),
+    def probe_total(parts, count):
+        return pl.pallas_call(
+            probe_kernel,
+            out_shape=jax.ShapeDtypeStruct((count, *piece.shape[1:]), jnp.float32),
+            in_specs=[VMEM],
+            out_specs=VMEM,
+            compiler_params=SMALL,
+            cost_estimate=URGENT,
+        )(parts)
+
+    parts = exchanged(probe_sums, "y")
+    parts = exchanged(probe_total(parts, depth), "z")
+    parts = exchanged(probe_total(parts, lax.axis_size(ROW)), ROW)
+
+    part_far = keep_far + lax.ppermute(send_far, "c", swap)
+    swapped = lax.ppermute(send_near, "c", swap)
+    crossed = lax.ppermute(part_far, "xl", swap)
+    band_share = jax.ShapeDtypeStruct((rows, *tile), jnp.float32)
+    own_share, to_paired, to_crossed = pl.pallas_call(
+        share_kernel,
+        out_shape=(band_share, band_share, band_share),
+        in_specs=[SMEM] + [VMEM] * 3,
+        out_specs=[VMEM] * 3,
+        compiler_params=SMALL,
+    )(odd, keep_near, swapped, crossed)
+    from_paired = lax.ppermute(to_paired, SCAN, pairs)
+    from_crossed = lax.ppermute(to_crossed, SCAN, others)
+    extra = piece.shape[1] // width
+    joined = pl.pallas_call(
+        join_kernel,
+        out_shape=jax.ShapeDtypeStruct((rows, layers + extra, width, size), jnp.float32),
+        in_specs=[VMEM] * 4,
+        out_specs=VMEM,
+        compiler_params=SMALL,
+    )(own_share, from_paired, from_crossed, parts)
+    object_gradient, probe_gradient = pl.pallas_call(
+        finish_kernel,
+        out_shape=(jax.ShapeDtypeStruct(own.shape, jnp.float32), piece),
         in_specs=[VMEM],
-        out_specs=VMEM,
-        compiler_params=SMALL,
-    )(exchanged(probe_part, PLANE))
-    probe_many = exchanged(probe_many, SCAN)
-
-    part_far = keep_far + lax.ppermute(send_far, "c", swap)
-    part_near = keep_near + lax.ppermute(send_near, "c", swap)
-    part = part_near + lax.ppermute(part_far, "xl", swap)
-    tile_out = jax.ShapeDtypeStruct(tile, jnp.float32)
-    own_sum, to_before, to_after, probe_many = pl.pallas_call(
-        finish_kernel,
-        out_shape=(tile_out, tile_out, tile_out, jax.ShapeDtypeStruct((plane, *bit), jnp.float32)),
-        in_specs=[VMEM] * 2,
-        out_specs=[VMEM] * 4,
-        compiler_params=SMALL,
-    )(exchanged(part, "y"), probe_many)
-
-    probe_mine = exchanged(probe_many, PLANE)
-    from_after = lax.ppermute(to_before, SCAN, down)
-    from_before = lax.ppermute(to_after, SCAN, up)
-    object_gradient, probe_mine = pl.pallas_call(
-        close_kernel,
-        out_shape=(
-            jax.ShapeDtypeStruct(own.shape, jnp.float32),
-            jax.ShapeDtypeStruct(probe_mine.shape, jnp.float32),
-        ),
-        in_specs=[VMEM] * 4,
-        out_specs=(VMEM, VMEM),
-        compiler_params=SMALL,
-    )(own_sum, from_after, from_before, probe_mine)
-    probe_theirs = lax.ppermute(probe_mine, "c", swap)
-    probe_gradient = pl.pallas_call(
-        merge_kernel,
-        out_shape=jax.ShapeDtypeStruct((plane, 2, *bit), jnp.float32),
-        in_specs=[SMEM, VMEM, VMEM],
-        out_specs=VMEM,
-        compiler_params=SMALL,
-    )(info, probe_mine, probe_theirs).reshape(probe.shape)
-    return (jnp.swapaxes(object_gradient, 2, 3), probe_gradient)
+        out_specs=[VMEM] * 2,
+        compiler_params=SMALL,
+    )(exchanged(joined, "y"))
+    return (jnp.swapaxes(object_gradient, 2, 3), probe_gradient.reshape(probe.shape))
 
 
 def solution(mesh):

time: 170 us -> 156 us (0.918); the launches traced: 167 us -> 155 us
  starting transfers between devices: 80.4 us -> 65.4 us
    ppermute x8 -> x6, waiting for transfers between devices: 3.72 us -> 15.8 us  [the longest x1 14.5 us: local(): crossed = lax.ppermute(part_far, 'xl', swap)]
    all_to_all x3, waiting for transfers between devices: 16.2 us -> 5.71 us  [exchanged(): return lax.all_to_all(array, axes, 0, 0, tiled=True)]
    ppermute x8 -> x6, starting transfers between devices: 28.8 us -> 19.8 us  [the longest x1 7.93 us: local(): paired = lax.ppermute(packed, SCAN, pairs)]
    ppermute x1, starting transfers between devices: 13.7 us -> 10.2 us  [local(): rim_theirs = lax.ppermute(rim_mine, 'c', swap)]
    all_to_all x3, starting transfers between devices: 33.8 us -> 30.9 us  [exchanged(): return lax.all_to_all(array, axes, 0, 0, tiled=True)]
  transfers between devices with their start and end apart: 14 -> 12, of which waited for: 7 -> 4; matrix products, arithmetic and copies ran while one was open for 0% -> 0% of each run, Pallas kernels for 0% -> 1%
where the time goes in v3:
time: 156 us; the launch traced here: 155 us
  starting transfers between devices  65.4 us (42%)
  blocking collectives  52.3 us (34%)
  waiting for transfers between devices  21.7 us (14%)
  Pallas kernels  11.2 us (7%)
  local copies, waits for them, and re-layouts  2.51 us (2%)
    all_to_all x3, blocking collectives, exchanged(): return lax.all_to_all(array, axes, 0, 0, tiled=True)  52.3 us
    all_to_all x3, starting transfers between devices, exchanged(): return lax.all_to_all(array, axes, 0, 0, tiled=True)  30.9 us
    ppermute x1, waiting for transfers between devices, local(): crossed = lax.ppermute(part_far, 'xl', swap)  14.5 us
    ppermute x1, starting transfers between devices, local(): rim_theirs = lax.ppermute(rim_mine, 'c', swap)  10.2 us
    pallas_call x1, Pallas kernels, local(): pl.pallas_call(gradient_kernel, out_shape=(share, share, share, share, pi...  8.67 us
    ppermute x1, starting transfers between devices, local(): paired = lax.ppermute(packed, SCAN, pairs)  7.93 us
    all_to_all x3, waiting for transfers between devices, exchanged(): return lax.all_to_all(array, axes, 0, 0, tiled=True)  5.71 us
    ppermute x1, starting transfers between devices, local(): from_paired = lax.ppermute(to_paired, SCAN, pairs)  4.12 us
  transfers between devices with their start and end apart: 12, of which 4 were waited for; matrix products, arithmetic and copies ran while one was open for 0% of the time, Pallas kernels for 1%

profile of v3, /device:TPU:1, one launch (start us, length us, event | category | flops | bytes accessed | tf_op | source)
XLA Modules:
  0.0 154.7 jit_solution(17933207146649811277)
XLA Ops:
  0.6 0.8 copy-done.4
  1.4 0.9 shard_map.95
  2.3 8.7 %all-to-all-start = ((f32[16,3,16,128]{3,2,1,0:T(8,128)}), f32[16,3,16,128]{3,2,1,0:T(8,128)S(1)}, u32[]{:S(2)}, u32[]{:S(2)}) async-start(f32[16,3,16,128]{3,2,1,0:T(8,128)} %get-tuple-element.14), calls=%async_computation | async-start | bytes 786432 | tf_op jit(solution)/shard_map/all_to_all | solution.py:232
  11.0 0.7 collective-permute-start.2
  11.6 7.9 %collective-permute-start.1 = (f32[3,16,128]{2,1,0:T(8,128)S(1)}, f32[3,16,128]{2,1,0:T(8,128)S(1)}, u32[]{:S(2)}, u32[]{:S(2)}) collective-permute-start(f32[3,16,128]{2,1,0:T(8,128)S(1)} %get-tuple-element.15), channel_id=1, source_target_pairs={{0,1},{1,0},{2,3},{3,2},{4,5},{5,4},{6,7},{7,6},{8,9},{9,8},{10,11... | collective-permute-start | bytes 73736 | tf_op jit(solution)/shard_map/ppermute | solution.py:273
  19.6 1.2 collective-permute-done.1.paired
  20.8 0.1 shard_map.96
  20.9 22.6 %all_to_all.30.rim_mine = f32[16,6,16,128]{3,2,1,0:T(8,128)S(1)} all-to-all(f32[16,6,16,128]{3,2,1,0:T(8,128)S(1)} %shard_map.96), channel_id=1, replica_groups=mesh['xl'=2,'y'=8,'c'=2,'z'=16,'xh'=2] {'xl','y'}, dimensions={0} | all-to-all | bytes 1572864 | tf_op jit(solution)/shard_map/all_to_all | solution.py:232
  43.5 10.2 %collective-permute-start.3 = (f32[16,6,16,128]{3,2,1,0:T(8,128)S(1)}, f32[16,6,16,128]{3,2,1,0:T(8,128)S(1)}, u32[]{:S(2)}, u32[]{:S(2)}) collective-permute-start(f32[16,6,16,128]{3,2,1,0:T(8,128)S(1)} %all_to_all.30.rim_mine), channel_id=1, source_target_pairs={{0,32},{32,0},{1,33},{33,1},{2,34},{34,2},{3,35},{35,3},{4,36},{36... | collective-permute-start | bytes 2359304 | tf_op jit(solution)/shard_map/ppermute | solution.py:284
  53.7 1.9 %collective-permute-start = (f32[16,3,16,128]{3,2,1,0:T(8,128)S(1)}, f32[16,3,16,128]{3,2,1,0:T(8,128)S(1)}, u32[]{:S(2)}, u32[]{:S(2)}) collective-permute-start(f32[16,3,16,128]{3,2,1,0:T(8,128)S(1)} %all-to-all-done.unused.own_mine), channel_id=1, source_target_pairs={{0,32},{32,0},{1,33},{33,1},{2,34},{34,2},{3,35},{35,3},{4,36},{36... | collective-permute-start | bytes 1179656 | tf_op jit(solution)/shard_map/ppermute | solution.py:282
  56.3 0.6 copy-done.8
  57.0 0.0 copy-done.9
  57.0 0.0 copy-done.10
  57.0 0.1 concatenate.3.info
  57.1 0.3 collective-permute-done.own_theirs
  57.4 0.9 copy-done.6
  58.3 8.7 %shard_map.97 = (f32[8,9,16,128]{3,2,1,0:T(8,128)}, f32[8,9,16,128]{3,2,1,0:T(8,128)}, f32[8,9,16,128]{3,2,1,0:T(8,128)}, f32[8,9,16,128]{3,2,1,0:T(8,128)}, f32[8,32,128]{2,1,0:T(8,128)}) custom-call(s32[10]{0:T(128)S(1)} %concatenate.3.info, bf16[2,2,2,128,128]{4,3,2,1,0:T(8,128)(2,1)S(1)} %copy-done.1, f32[2,128,128]{2,1,0:T(8,128)S(1)} %copy-done.2, ...), custom_call_target="tpu_custom_call" | custom-call | tf_op jit(solution)/shard_map/pallas_call | solution.py:290
  67.0 3.9 %all-to-all-start.2 = ((f32[8,32,128]{2,1,0:T(8,128)}), f32[8,32,128]{2,1,0:T(8,128)S(1)}, u32[]{:S(2)}, u32[]{:S(2)}) async-start(f32[8,32,128]{2,1,0:T(8,128)} %get-tuple-element.23), calls=%async_computation.2 | async-start | bytes 262144 | tf_op jit(solution)/shard_map/all_to_all | solution.py:232
  70.9 2.5 %collective-permute-start.5 = (f32[8,9,16,128]{3,2,1,0:T(8,128)}, f32[8,9,16,128]{3,2,1,0:T(8,128)S(1)}, u32[]{:S(2)}, u32[]{:S(2)}) collective-permute-start(f32[8,9,16,128]{3,2,1,0:T(8,128)} %get-tuple-element.19), channel_id=1, source_target_pairs={{0,32},{32,0},{1,33},{33,1},{2,34},{34,2},{3,35},{35,3},{4,36},{36... | collective-permute-start | bytes 1769480 | tf_op jit(solution)/shard_map/ppermute | solution.py:322
  73.4 5.7 %all-to-all-done.2.parts = f32[8,32,128]{2,1,0:T(8,128)S(1)} async-done(((f32[8,32,128]{2,1,0:T(8,128)}), f32[8,32,128]{2,1,0:T(8,128)S(1)}, u32[]{:S(2)}, u32[]{:S(2)}) %all-to-all-start.2) | async-done | bytes 131104 | tf_op jit(solution)/shard_map/all_to_all | solution.py:232
  79.1 0.7 shard_map.99
  79.9 18.3 %all-to-all-start.3 = ((f32[16,32,128]{2,1,0:T(8,128)}), f32[16,32,128]{2,1,0:T(8,128)S(1)}, u32[]{:S(2)}, u32[]{:S(2)}) async-start(f32[16,32,128]{2,1,0:T(8,128)} %shard_map.99), calls=%async_computation.3 | async-start | bytes 524288 | tf_op jit(solution)/shard_map/all_to_all | solution.py:232
  98.2 4.0 %collective-permute-start.4 = (f32[8,9,16,128]{3,2,1,0:T(8,128)S(1)}, f32[8,9,16,128]{3,2,1,0:T(8,128)S(1)}, u32[]{:S(2)}, u32[]{:S(2)}) collective-permute-start(f32[8,9,16,128]{3,2,1,0:T(8,128)S(1)} %copy-done.11), channel_id=1, source_target_pairs={{0,32},{32,0},{1,33},{33,1},{2,34},{34,2},{3,35},{35,3},{4,36},{36... | collective-permute-start | bytes 1769480 | tf_op jit(solution)/shard_map/ppermute | solution.py:323
  102.3 0.1 add.3
  102.3 2.4 %collective-permute-start.6 = (f32[8,9,16,128]{3,2,1,0:T(8,128)S(1)}, f32[8,9,16,128]{3,2,1,0:T(8,128)S(1)}, u32[]{:S(2)}, u32[]{:S(2)}) collective-permute-start(f32[8,9,16,128]{3,2,1,0:T(8,128)S(1)} %add.3), channel_id=1, source_target_pairs={{0,512},{512,0},{1,513},{513,1},{2,514},{514,2},{3,515},{515,3},{4... | collective-permute-start | bytes 1769480 | tf_op jit(solution)/shard_map/ppermute | solution.py:324
  104.8 14.5 %collective-permute-done.6.crossed = f32[8,9,16,128]{3,2,1,0:T(8,128)S(1)} collective-permute-done((f32[8,9,16,128]{3,2,1,0:T(8,128)S(1)}, f32[8,9,16,128]{3,2,1,0:T(8,128)S(1)}, u32[]{:S(2)}, u32[]{:S(2)}) %collective-permute-start.6) | collective-permute-done | bytes 589856 | tf_op jit(solution)/shard_map/ppermute | solution.py:324
  119.3 0.1 shard_map.98
  119.4 4.1 %collective-permute-start.7 = (f32[8,3,16,128]{3,2,1,0:T(8,128)S(1)}, f32[8,3,16,128]{3,2,1,0:T(8,128)S(1)}, u32[]{:S(2)}, u32[]{:S(2)}) collective-permute-start(f32[8,3,16,128]{3,2,1,0:T(8,128)S(1)} %get-tuple-element.21), channel_id=1, source_target_pairs={{0,1},{1,0},{2,3},{3,2},{4,5},{5,4},{6,7},{7,6},{8,9},{9,8},{10,11... | collective-permute-start | bytes 589832 | tf_op jit(solution)/shard_map/ppermute | solution.py:333
  123.6 0.7 collective-permute-start.8
  124.3 13.5 %all_to_all.31.parts = f32[8,32,128]{2,1,0:T(8,128)S(1)} all-to-all(f32[8,32,128]{2,1,0:T(8,128)S(1)} %shard_map.100), channel_id=1, replica_groups=mesh['xl'=2,'y'=8,'c'=2,'z'=16,'xh'=2] {'xl','c','xh'}, dimensions={0} | all-to-all | bytes 262144 | tf_op jit(solution)/shard_map/all_to_all | solution.py:232
  137.9 16.1 %all_to_all.32.shares = f32[8,5,16,128]{3,2,1,0:T(8,128)S(1)} all-to-all(f32[8,5,16,128]{3,2,1,0:T(8,128)S(1)} %shard_map.101), channel_id=1, replica_groups=mesh['xl'=2,'y'=8,'c'=2,'z'=16,'xh'=2] {'y'}, dimensions={0} | all-to-all | bytes 655360 | tf_op jit(solution)/shard_map/all_to_all | solution.py:232
  154.0 0.7 shard_map.102
  (29 shorter events, 0.1 us)
Async XLA Ops:
  0.6 0.8 copy-start.4
  2.3 18.5 %all-to-all-start = ((f32[16,3,16,128]{3,2,1,0:T(8,128)}), f32[16,3,16,128]{3,2,1,0:T(8,128)S(1)}, u32[]{:S(2)}, u32[]{:S(2)}) async-start(f32[16,3,16,128]{3,2,1,0:T(8,128)} %get-tuple-element.14), calls=%async_computation | async-start | bytes 786432 | tf_op jit(solution)/shard_map/all_to_all | solution.py:232
  11.0 8.6 %collective-permute-start.2 = (f32[3,16,128]{2,1,0:T(8,128)S(1)}, f32[3,16,128]{2,1,0:T(8,128)S(1)}, u32[]{:S(2)}, u32[]{:S(2)}) collective-permute-start(f32[3,16,128]{2,1,0:T(8,128)S(1)} %get-tuple-element.15), channel_id=1, source_target_pairs={{1,2},{2,1},{3,4},{4,3},{5,6},{6,5},{7,8},{8,7},{9,10},{10,9},{11,... | collective-permute-start | bytes 73736 | tf_op jit(solution)/shard_map/ppermute | solution.py:274
  11.6 9.2 %collective-permute-start.1 = (f32[3,16,128]{2,1,0:T(8,128)S(1)}, f32[3,16,128]{2,1,0:T(8,128)S(1)}, u32[]{:S(2)}, u32[]{:S(2)}) collective-permute-start(f32[3,16,128]{2,1,0:T(8,128)S(1)} %get-tuple-element.15), channel_id=1, source_target_pairs={{0,1},{1,0},{2,3},{3,2},{4,5},{5,4},{6,7},{7,6},{8,9},{9,8},{10,11... | collective-permute-start | bytes 73736 | tf_op jit(solution)/shard_map/ppermute | solution.py:273
  20.9 37.4 %copy-start.1 = (bf16[2,2,2,128,128]{4,3,2,1,0:T(8,128)(2,1)S(1)}, bf16[2,2,2,128,128]{4,3,2,1,0:T(8,128)(2,1)}, u32[]{:S(2)}) copy-start(bf16[2,2,2,128,128]{4,3,2,1,0:T(8,128)(2,1)} %constant.14.clone.table) | copy-start | bytes 786436
  20.9 37.4 %copy-start.2 = (f32[2,128,128]{2,1,0:T(8,128)S(1)}, f32[2,128,128]{2,1,0:T(8,128)}, u32[]{:S(2)}) copy-start(f32[2,128,128]{2,1,0:T(8,128)} %probe.1) | copy-start | bytes 393220
  20.9 37.4 %copy-start.3 = (f32[1,1,2,128,128]{4,3,2,1,0:T(8,128)S(1)}, f32[1,1,2,128,128]{4,3,2,1,0:T(8,128)}, u32[]{:S(2)}) copy-start(f32[1,1,2,128,128]{4,3,2,1,0:T(8,128)} %param.10) | copy-start | bytes 393220
  43.5 13.8 %copy-start.5 = (f32[16,6,16,128]{3,2,1,0:T(8,128)}, f32[16,6,16,128]{3,2,1,0:T(8,128)S(1)}, u32[]{:S(2)}) copy-start(f32[16,6,16,128]{3,2,1,0:T(8,128)S(1)} %all_to_all.30.rim_mine) | copy-start | bytes 2359300
  43.5 13.8 %collective-permute-start.3 = (f32[16,6,16,128]{3,2,1,0:T(8,128)S(1)}, f32[16,6,16,128]{3,2,1,0:T(8,128)S(1)}, u32[]{:S(2)}, u32[]{:S(2)}) collective-permute-start(f32[16,6,16,128]{3,2,1,0:T(8,128)S(1)} %all_to_all.30.rim_mine), channel_id=1, source_target_pairs={{0,32},{32,0},{1,33},{33,1},{2,34},{34,2},{3,35},{35,3},{4,36},{36... | collective-permute-start | bytes 2359304 | tf_op jit(solution)/shard_map/ppermute | solution.py:284
  53.7 3.6 %collective-permute-start = (f32[16,3,16,128]{3,2,1,0:T(8,128)S(1)}, f32[16,3,16,128]{3,2,1,0:T(8,128)S(1)}, u32[]{:S(2)}, u32[]{:S(2)}) collective-permute-start(f32[16,3,16,128]{3,2,1,0:T(8,128)S(1)} %all-to-all-done.unused.own_mine), channel_id=1, source_target_pairs={{0,32},{32,0},{1,33},{33,1},{2,34},{34,2},{3,35},{35,3},{4,36},{36... | collective-permute-start | bytes 1179656 | tf_op jit(solution)/shard_map/ppermute | solution.py:282
  56.3 0.7 copy-start.8
  56.3 0.7 copy-start.9
  56.3 0.7 copy-start.10
  57.3 0.9 copy-start.6
  67.0 12.2 %all-to-all-start.2 = ((f32[8,32,128]{2,1,0:T(8,128)}), f32[8,32,128]{2,1,0:T(8,128)S(1)}, u32[]{:S(2)}, u32[]{:S(2)}) async-start(f32[8,32,128]{2,1,0:T(8,128)} %get-tuple-element.23), calls=%async_computation.2 | async-start | bytes 262144 | tf_op jit(solution)/shard_map/all_to_all | solution.py:232
  70.9 27.3 %copy-start.11 = (f32[8,9,16,128]{3,2,1,0:T(8,128)S(1)}, f32[8,9,16,128]{3,2,1,0:T(8,128)}, u32[]{:S(2)}) copy-start(f32[8,9,16,128]{3,2,1,0:T(8,128)} %get-tuple-element.17) | copy-start | bytes 1769476
  70.9 31.3 %collective-permute-start.5 = (f32[8,9,16,128]{3,2,1,0:T(8,128)}, f32[8,9,16,128]{3,2,1,0:T(8,128)S(1)}, u32[]{:S(2)}, u32[]{:S(2)}) collective-permute-start(f32[8,9,16,128]{3,2,1,0:T(8,128)} %get-tuple-element.19), channel_id=1, source_target_pairs={{0,32},{32,0},{1,33},{33,1},{2,34},{34,2},{3,35},{35,3},{4,36},{36... | collective-permute-start | bytes 1769480 | tf_op jit(solution)/shard_map/ppermute | solution.py:322
  79.1 23.1 %copy-start.7 = (f32[8,9,16,128]{3,2,1,0:T(8,128)S(1)}, f32[8,9,16,128]{3,2,1,0:T(8,128)}, u32[]{:S(2)}) copy-start(f32[8,9,16,128]{3,2,1,0:T(8,128)} %get-tuple-element.18) | copy-start | bytes 1769476
  79.9 44.4 %all-to-all-start.3 = ((f32[16,32,128]{2,1,0:T(8,128)}), f32[16,32,128]{2,1,0:T(8,128)S(1)}, u32[]{:S(2)}, u32[]{:S(2)}) async-start(f32[16,32,128]{2,1,0:T(8,128)} %shard_map.99), calls=%async_computation.3 | async-start | bytes 524288 | tf_op jit(solution)/shard_map/all_to_all | solution.py:232
  98.2 6.6 %collective-permute-start.4 = (f32[8,9,16,128]{3,2,1,0:T(8,128)S(1)}, f32[8,9,16,128]{3,2,1,0:T(8,128)S(1)}, u32[]{:S(2)}, u32[]{:S(2)}) collective-permute-start(f32[8,9,16,128]{3,2,1,0:T(8,128)S(1)} %copy-done.11), channel_id=1, source_target_pairs={{0,32},{32,0},{1,33},{33,1},{2,34},{34,2},{3,35},{35,3},{4,36},{36... | collective-permute-start | bytes 1769480 | tf_op jit(solution)/shard_map/ppermute | solution.py:323
  102.2 17.1 %copy-start = (f32[8,9,16,128]{3,2,1,0:T(8,128)S(1)}, f32[8,9,16,128]{3,2,1,0:T(8,128)}, u32[]{:S(2)}) copy-start(f32[8,9,16,128]{3,2,1,0:T(8,128)} %get-tuple-element.16.kept) | copy-start | bytes 1769476
  102.3 17.0 %collective-permute-start.6 = (f32[8,9,16,128]{3,2,1,0:T(8,128)S(1)}, f32[8,9,16,128]{3,2,1,0:T(8,128)S(1)}, u32[]{:S(2)}, u32[]{:S(2)}) collective-permute-start(f32[8,9,16,128]{3,2,1,0:T(8,128)S(1)} %add.3), channel_id=1, source_target_pairs={{0,512},{512,0},{1,513},{513,1},{2,514},{514,2},{3,515},{515,3},{4... | collective-permute-start | bytes 1769480 | tf_op jit(solution)/shard_map/ppermute | solution.py:324
  119.4 18.4 %collective-permute-start.7 = (f32[8,3,16,128]{3,2,1,0:T(8,128)S(1)}, f32[8,3,16,128]{3,2,1,0:T(8,128)S(1)}, u32[]{:S(2)}, u32[]{:S(2)}) collective-permute-start(f32[8,3,16,128]{3,2,1,0:T(8,128)S(1)} %get-tuple-element.21), channel_id=1, source_target_pairs={{0,1},{1,0},{2,3},{3,2},{4,5},{5,4},{6,7},{7,6},{8,9},{9,8},{10,11... | collective-permute-start | bytes 589832 | tf_op jit(solution)/shard_map/ppermute | solution.py:333
  123.6 14.3 %collective-permute-start.8 = (f32[8,3,16,128]{3,2,1,0:T(8,128)S(1)}, f32[8,3,16,128]{3,2,1,0:T(8,128)S(1)}, u32[]{:S(2)}, u32[]{:S(2)}) collective-permute-start(f32[8,3,16,128]{3,2,1,0:T(8,128)S(1)} %get-tuple-element.22), channel_id=1, source_target_pairs={{1,2},{2,1},{3,4},{4,3},{5,6},{6,5},{7,8},{8,7},{9,10},{10,9},{11,... | collective-permute-start | bytes 589832 | tf_op jit(solution)/shard_map/ppermute | solution.py:334

commit v4 on v3

--- a/solution.py
+++ b/solution.py
@@ -289,7 +289,7 @@
     table = jnp.asarray(tables(size))
     keep_near, keep_far, send_near, send_far, probe_sums = pl.pallas_call(
         gradient_kernel,
-        out_shape=(share, share, share, share, piece),
+        out_shape=(share, share, *[pltpu.HBM(x.shape, x.dtype) for x in (share, share, piece)]),
         in_specs=[SMEM] + [HBM] * 3 + [ANY] * 4,
         out_specs=[HBM] * 5,
         scratch_shapes=[
@@ -302,26 +302,26 @@
             pltpu.SemaphoreType.DMA((2 * groups + 3,)),
             pltpu.SemaphoreType.DMA((4 * groups + 1,)),
         ],
-        compiler_params=pltpu.CompilerParams(vmem_limit_bytes=52 * 1024 * 1024),
+        compiler_params=pltpu.CompilerParams(vmem_limit_bytes=32 * 1024 * 1024),
     )(info, table, probe, intensities[0, 0], own_mine, own_theirs, rim_mine, rim_theirs)
 
-    def probe_total(parts, count):
+    def probe_total(parts, count, cost=None):
         return pl.pallas_call(
             probe_kernel,
             out_shape=jax.ShapeDtypeStruct((count, *piece.shape[1:]), jnp.float32),
             in_specs=[VMEM],
             out_specs=VMEM,
             compiler_params=SMALL,
-            cost_estimate=URGENT,
+            cost_estimate=cost,
         )(parts)
 
     parts = exchanged(probe_sums, "y")
-    parts = exchanged(probe_total(parts, depth), "z")
-    parts = exchanged(probe_total(parts, lax.axis_size(ROW)), ROW)
-
     part_far = keep_far + lax.ppermute(send_far, "c", swap)
     swapped = lax.ppermute(send_near, "c", swap)
     crossed = lax.ppermute(part_far, "xl", swap)
+    parts = probe_total(parts, depth)
+    parts, crossed, swapped = lax.optimization_barrier((parts, crossed, swapped))
+    parts = exchanged(parts, "z")
     band_share = jax.ShapeDtypeStruct((rows, *tile), jnp.float32)
     own_share, to_paired, to_crossed = pl.pallas_call(
         share_kernel,
@@ -330,6 +330,7 @@
         out_specs=[VMEM] * 3,
         compiler_params=SMALL,
     )(odd, keep_near, swapped, crossed)
+    parts = exchanged(probe_total(parts, lax.axis_size(ROW)), ROW)
     from_paired = lax.ppermute(to_paired, SCAN, pairs)
     from_crossed = lax.ppermute(to_crossed, SCAN, others)
     extra = piece.shape[1] // width

time: 156 us -> 152 us (0.974)
  starting transfers between devices: 65.4 us -> 70.5 us
  waiting for transfers between devices: 21.7 us -> 16.8 us
  blocking collectives: 52.3 us -> 50.3 us
    ppermute x1, waiting for transfers between devices: 14.5 us -> 1.99 us  [local(): crossed = lax.ppermute(part_far, 'xl', swap)]
    all_to_all x3, waiting for transfers between devices: 5.71 us -> 13.4 us  [exchanged(): return lax.all_to_all(array, axes, 0, 0, tiled=True)]
    all_to_all x3, starting transfers between devices: 30.9 us -> 38 us  [exchanged(): return lax.all_to_all(array, axes, 0, 0, tiled=True)]
    all_to_all x3, blocking collectives: 52.3 us -> 50.3 us  [exchanged(): return lax.all_to_all(array, axes, 0, 0, tiled=True)]
    ppermute x1, starting transfers between devices: 4.02 us -> 2.16 us  [local(): swapped = lax.ppermute(send_near, 'c', swap)]
  transfers between devices with their start and end apart: 12 -> 12, of which waited for: 4 -> 5; matrix products, arithmetic and copies ran while one was open for 0% -> 0% of each run, Pallas kernels for 1% -> 1%
where the time goes in v4:
time: 152 us; the launch traced here: 151 us
  starting transfers between devices  70.5 us (46%)
  blocking collectives  50.3 us (33%)
  waiting for transfers between devices  16.8 us (11%)
  Pallas kernels  10.4 us (7%)
  local copies, waits for them, and re-layouts  1.56 us (1%)
  between operations  1.52 us (1%)
    all_to_all x3, blocking collectives, exchanged(): return lax.all_to_all(array, axes, 0, 0, tiled=True)  50.3 us
    all_to_all x3, starting transfers between devices, exchanged(): return lax.all_to_all(array, axes, 0, 0, tiled=True)  38 us
    all_to_all x3, waiting for transfers between devices, exchanged(): return lax.all_to_all(array, axes, 0, 0, tiled=True)  13.4 us
    ppermute x1, starting transfers between devices, local(): rim_theirs = lax.ppermute(rim_mine, 'c', swap)  10.2 us
    ppermute x1, starting transfers between devices, local(): paired = lax.ppermute(packed, SCAN, pairs)  7.93 us
    pallas_call x1, Pallas kernels, local(): pl.pallas_call(gradient_kernel, out_shape=(share, share, *[pltpu.HBM(x.sh...  7.26 us
    ppermute x1, starting transfers between devices, local(): from_paired = lax.ppermute(to_paired, SCAN, pairs)  4.07 us
  transfers between devices with their start and end apart: 12, of which 5 were waited for; matrix products, arithmetic and copies ran while one was open for 0% of the time, Pallas kernels for 1%

profile of v4, /device:TPU:1, one launch (start us, length us, event | category | flops | bytes accessed | tf_op | source)
XLA Modules:
  0.0 151.2 jit_solution(1580050321391316338)
XLA Ops:
  0.6 0.8 copy-done.3
  1.4 0.8 shard_map.95
  2.3 8.7 %all-to-all-start = ((f32[16,3,16,128]{3,2,1,0:T(8,128)}), f32[16,3,16,128]{3,2,1,0:T(8,128)S(1)}, u32[]{:S(2)}, u32[]{:S(2)}) async-start(f32[16,3,16,128]{3,2,1,0:T(8,128)} %get-tuple-element.17), calls=%async_computation | async-start | bytes 786432 | tf_op jit(solution)/shard_map/all_to_all | solution.py:232
  11.0 0.7 collective-permute-start.2
  11.6 7.9 %collective-permute-start.1 = (f32[3,16,128]{2,1,0:T(8,128)S(1)}, f32[3,16,128]{2,1,0:T(8,128)S(1)}, u32[]{:S(2)}, u32[]{:S(2)}) collective-permute-start(f32[3,16,128]{2,1,0:T(8,128)S(1)} %get-tuple-element.18), channel_id=1, source_target_pairs={{0,1},{1,0},{2,3},{3,2},{4,5},{5,4},{6,7},{7,6},{8,9},{9,8},{10,11... | collective-permute-start | bytes 73736 | tf_op jit(solution)/shard_map/ppermute | solution.py:273
  19.6 1.2 collective-permute-done.1.paired
  20.8 0.1 shard_map.96
  20.9 22.6 %all_to_all.30.rim_mine = f32[16,6,16,128]{3,2,1,0:T(8,128)S(1)} all-to-all(f32[16,6,16,128]{3,2,1,0:T(8,128)S(1)} %shard_map.96), channel_id=1, replica_groups=mesh['xl'=2,'y'=8,'c'=2,'z'=16,'xh'=2] {'xl','y'}, dimensions={0} | all-to-all | bytes 1572864 | tf_op jit(solution)/shard_map/all_to_all | solution.py:232
  43.5 10.2 %collective-permute-start.3 = (f32[16,6,16,128]{3,2,1,0:T(8,128)S(1)}, f32[16,6,16,128]{3,2,1,0:T(8,128)S(1)}, u32[]{:S(2)}, u32[]{:S(2)}) collective-permute-start(f32[16,6,16,128]{3,2,1,0:T(8,128)S(1)} %all_to_all.30.rim_mine), channel_id=1, source_target_pairs={{0,32},{32,0},{1,33},{33,1},{2,34},{34,2},{3,35},{35,3},{4,36},{36... | collective-permute-start | bytes 2359304 | tf_op jit(solution)/shard_map/ppermute | solution.py:284
  53.7 1.9 %collective-permute-start = (f32[16,3,16,128]{3,2,1,0:T(8,128)S(1)}, f32[16,3,16,128]{3,2,1,0:T(8,128)S(1)}, u32[]{:S(2)}, u32[]{:S(2)}) collective-permute-start(f32[16,3,16,128]{3,2,1,0:T(8,128)S(1)} %all-to-all-done.unused.own_mine), channel_id=1, source_target_pairs={{0,32},{32,0},{1,33},{33,1},{2,34},{34,2},{3,35},{35,3},{4,36},{36... | collective-permute-start | bytes 1179656 | tf_op jit(solution)/shard_map/ppermute | solution.py:282
  56.3 0.6 copy-done.5
  57.0 0.0 copy-done.6
  57.0 0.1 concatenate.3.info
  57.1 0.3 collective-permute-done.own_theirs
  57.4 7.3 %shard_map.97 = (f32[8,9,16,128]{3,2,1,0:T(8,128)S(1)}, f32[8,9,16,128]{3,2,1,0:T(8,128)S(1)}, f32[8,9,16,128]{3,2,1,0:T(8,128)}, f32[8,9,16,128]{3,2,1,0:T(8,128)}, f32[8,32,128]{2,1,0:T(8,128)}) custom-call(s32[10]{0:T(128)S(1)} %concatenate.3.info, bf16[2,2,2,128,128]{4,3,2,1,0:T(8,128)(2,1)S(1)} %copy-done, f32[2,128,128]{2,1,0:T(8,128)S(1)} %copy-done.1, ...), custom_call_target="tpu_custom_call" | custom-call | tf_op jit(solution)/shard_map/pallas_call | solution.py:290
  64.6 2.2 %collective-permute-start.4 = (f32[8,9,16,128]{3,2,1,0:T(8,128)}, f32[8,9,16,128]{3,2,1,0:T(8,128)S(1)}, u32[]{:S(2)}, u32[]{:S(2)}) collective-permute-start(f32[8,9,16,128]{3,2,1,0:T(8,128)} %get-tuple-element.22), channel_id=1, source_target_pairs={{0,32},{32,0},{1,33},{33,1},{2,34},{34,2},{3,35},{35,3},{4,36},{36... | collective-permute-start | bytes 1769480 | tf_op jit(solution)/shard_map/ppermute | solution.py:319
  66.8 2.2 %collective-permute-start.6 = (f32[8,9,16,128]{3,2,1,0:T(8,128)}, f32[8,9,16,128]{3,2,1,0:T(8,128)S(1)}, u32[]{:S(2)}, u32[]{:S(2)}) collective-permute-start(f32[8,9,16,128]{3,2,1,0:T(8,128)} %get-tuple-element.23), channel_id=1, source_target_pairs={{0,32},{32,0},{1,33},{33,1},{2,34},{34,2},{3,35},{35,3},{4,36},{36... | collective-permute-start | bytes 1769480 | tf_op jit(solution)/shard_map/ppermute | solution.py:320
  69.0 0.1 add.3
  69.1 2.7 %collective-permute-start.5 = (f32[8,9,16,128]{3,2,1,0:T(8,128)S(1)}, f32[8,9,16,128]{3,2,1,0:T(8,128)S(1)}, u32[]{:S(2)}, u32[]{:S(2)}) collective-permute-start(f32[8,9,16,128]{3,2,1,0:T(8,128)S(1)} %add.3), channel_id=1, source_target_pairs={{0,512},{512,0},{1,513},{513,1},{2,514},{514,2},{3,515},{515,3},{4... | collective-permute-start | bytes 1769480 | tf_op jit(solution)/shard_map/ppermute | solution.py:321
  71.8 11.1 %all_to_all.31.parts = f32[8,32,128]{2,1,0:T(8,128)S(1)} all-to-all(f32[8,32,128]{2,1,0:T(8,128)S(1)} %copy-done.4), channel_id=1, replica_groups=mesh['xl'=2,'y'=8,'c'=2,'z'=16,'xh'=2] {'y'}, dimensions={0} | all-to-all | bytes 262144 | tf_op jit(solution)/shard_map/all_to_all | solution.py:232
  82.9 0.8 shard_map.98
  83.6 2.0 %collective-permute-done.5.crossed = f32[8,9,16,128]{3,2,1,0:T(8,128)S(1)} collective-permute-done((f32[8,9,16,128]{3,2,1,0:T(8,128)S(1)}, f32[8,9,16,128]{3,2,1,0:T(8,128)S(1)}, u32[]{:S(2)}, u32[]{:S(2)}) %collective-permute-start.5) | collective-permute-done | bytes 589856 | tf_op jit(solution)/shard_map/ppermute | solution.py:321
  85.6 18.3 %all-to-all-start.3 = ((f32[16,32,128]{2,1,0:T(8,128)}), f32[16,32,128]{2,1,0:T(8,128)S(1)}, u32[]{:S(2)}, u32[]{:S(2)}) async-start(f32[16,32,128]{2,1,0:T(8,128)} %shard_map.98), calls=%async_computation.3 | async-start | bytes 524288 | tf_op jit(solution)/shard_map/all_to_all | solution.py:232
  103.9 0.1 shard_map.99
  104.0 4.1 %collective-permute-start.7 = (f32[8,3,16,128]{3,2,1,0:T(8,128)S(1)}, f32[8,3,16,128]{3,2,1,0:T(8,128)S(1)}, u32[]{:S(2)}, u32[]{:S(2)}) collective-permute-start(f32[8,3,16,128]{3,2,1,0:T(8,128)S(1)} %get-tuple-element.27), channel_id=1, source_target_pairs={{0,1},{1,0},{2,3},{3,2},{4,5},{5,4},{6,7},{7,6},{8,9},{9,8},{10,11... | collective-permute-start | bytes 589832 | tf_op jit(solution)/shard_map/ppermute | solution.py:334
  108.1 0.7 collective-permute-start.8
  108.8 8.1 %all-to-all-done.3.parts = f32[16,32,128]{2,1,0:T(8,128)S(1)} async-done(((f32[16,32,128]{2,1,0:T(8,128)}), f32[16,32,128]{2,1,0:T(8,128)S(1)}, u32[]{:S(2)}, u32[]{:S(2)}) %all-to-all-start.3) | async-done | bytes 262176 | tf_op jit(solution)/shard_map/all_to_all | solution.py:232
  116.9 0.7 shard_map.100
  117.6 11.0 %all-to-all-start.4 = ((f32[8,32,128]{2,1,0:T(8,128)}), f32[8,32,128]{2,1,0:T(8,128)S(1)}, u32[]{:S(2)}, u32[]{:S(2)}) async-start(f32[8,32,128]{2,1,0:T(8,128)} %shard_map.100), calls=%async_computation.4 | async-start | bytes 262144 | tf_op jit(solution)/shard_map/all_to_all | solution.py:232
  128.6 5.3 %all-to-all-done.4.parts = f32[8,32,128]{2,1,0:T(8,128)S(1)} async-done(((f32[8,32,128]{2,1,0:T(8,128)}), f32[8,32,128]{2,1,0:T(8,128)S(1)}, u32[]{:S(2)}, u32[]{:S(2)}) %all-to-all-start.4) | async-done | bytes 131104 | tf_op jit(solution)/shard_map/all_to_all | solution.py:232
  133.9 16.6 %all_to_all.32.shares = f32[8,5,16,128]{3,2,1,0:T(8,128)S(1)} all-to-all(f32[8,5,16,128]{3,2,1,0:T(8,128)S(1)} %shard_map.101), channel_id=1, replica_groups=mesh['xl'=2,'y'=8,'c'=2,'z'=16,'xh'=2] {'y'}, dimensions={0} | all-to-all | bytes 655360 | tf_op jit(solution)/shard_map/all_to_all | solution.py:232
  150.5 0.7 shard_map.102
  (21 shorter events, 0.1 us)
Async XLA Ops:
  0.6 0.8 copy-start.3
  2.3 18.5 %all-to-all-start = ((f32[16,3,16,128]{3,2,1,0:T(8,128)}), f32[16,3,16,128]{3,2,1,0:T(8,128)S(1)}, u32[]{:S(2)}, u32[]{:S(2)}) async-start(f32[16,3,16,128]{3,2,1,0:T(8,128)} %get-tuple-element.17), calls=%async_computation | async-start | bytes 786432 | tf_op jit(solution)/shard_map/all_to_all | solution.py:232
  11.0 8.6 %collective-permute-start.2 = (f32[3,16,128]{2,1,0:T(8,128)S(1)}, f32[3,16,128]{2,1,0:T(8,128)S(1)}, u32[]{:S(2)}, u32[]{:S(2)}) collective-permute-start(f32[3,16,128]{2,1,0:T(8,128)S(1)} %get-tuple-element.18), channel_id=1, source_target_pairs={{1,2},{2,1},{3,4},{4,3},{5,6},{6,5},{7,8},{8,7},{9,10},{10,9},{11,... | collective-permute-start | bytes 73736 | tf_op jit(solution)/shard_map/ppermute | solution.py:274
  11.6 9.2 %collective-permute-start.1 = (f32[3,16,128]{2,1,0:T(8,128)S(1)}, f32[3,16,128]{2,1,0:T(8,128)S(1)}, u32[]{:S(2)}, u32[]{:S(2)}) collective-permute-start(f32[3,16,128]{2,1,0:T(8,128)S(1)} %get-tuple-element.18), channel_id=1, source_target_pairs={{0,1},{1,0},{2,3},{3,2},{4,5},{5,4},{6,7},{7,6},{8,9},{9,8},{10,11... | collective-permute-start | bytes 73736 | tf_op jit(solution)/shard_map/ppermute | solution.py:273
  20.9 36.4 %copy-start = (bf16[2,2,2,128,128]{4,3,2,1,0:T(8,128)(2,1)S(1)}, bf16[2,2,2,128,128]{4,3,2,1,0:T(8,128)(2,1)}, u32[]{:S(2)}) copy-start(bf16[2,2,2,128,128]{4,3,2,1,0:T(8,128)(2,1)} %constant.14.clone.table) | copy-start | bytes 786436
  20.9 36.4 %copy-start.1 = (f32[2,128,128]{2,1,0:T(8,128)S(1)}, f32[2,128,128]{2,1,0:T(8,128)}, u32[]{:S(2)}) copy-start(f32[2,128,128]{2,1,0:T(8,128)} %probe.1) | copy-start | bytes 393220
  20.9 36.4 %copy-start.2 = (f32[1,1,2,128,128]{4,3,2,1,0:T(8,128)S(1)}, f32[1,1,2,128,128]{4,3,2,1,0:T(8,128)}, u32[]{:S(2)}) copy-start(f32[1,1,2,128,128]{4,3,2,1,0:T(8,128)} %param.10) | copy-start | bytes 393220
  43.5 13.8 %collective-permute-start.3 = (f32[16,6,16,128]{3,2,1,0:T(8,128)S(1)}, f32[16,6,16,128]{3,2,1,0:T(8,128)S(1)}, u32[]{:S(2)}, u32[]{:S(2)}) collective-permute-start(f32[16,6,16,128]{3,2,1,0:T(8,128)S(1)} %all_to_all.30.rim_mine), channel_id=1, source_target_pairs={{0,32},{32,0},{1,33},{33,1},{2,34},{34,2},{3,35},{35,3},{4,36},{36... | collective-permute-start | bytes 2359304 | tf_op jit(solution)/shard_map/ppermute | solution.py:284
  53.7 3.6 %collective-permute-start = (f32[16,3,16,128]{3,2,1,0:T(8,128)S(1)}, f32[16,3,16,128]{3,2,1,0:T(8,128)S(1)}, u32[]{:S(2)}, u32[]{:S(2)}) collective-permute-start(f32[16,3,16,128]{3,2,1,0:T(8,128)S(1)} %all-to-all-done.unused.own_mine), channel_id=1, source_target_pairs={{0,32},{32,0},{1,33},{33,1},{2,34},{34,2},{3,35},{35,3},{4,36},{36... | collective-permute-start | bytes 1179656 | tf_op jit(solution)/shard_map/ppermute | solution.py:282
  56.3 0.7 copy-start.5
  56.3 0.7 copy-start.6
  56.3 0.7 copy-start.7
  64.6 4.3 %collective-permute-start.4 = (f32[8,9,16,128]{3,2,1,0:T(8,128)}, f32[8,9,16,128]{3,2,1,0:T(8,128)S(1)}, u32[]{:S(2)}, u32[]{:S(2)}) collective-permute-start(f32[8,9,16,128]{3,2,1,0:T(8,128)} %get-tuple-element.22), channel_id=1, source_target_pairs={{0,32},{32,0},{1,33},{33,1},{2,34},{34,2},{3,35},{35,3},{4,36},{36... | collective-permute-start | bytes 1769480 | tf_op jit(solution)/shard_map/ppermute | solution.py:319
  66.8 16.9 %collective-permute-start.6 = (f32[8,9,16,128]{3,2,1,0:T(8,128)}, f32[8,9,16,128]{3,2,1,0:T(8,128)S(1)}, u32[]{:S(2)}, u32[]{:S(2)}) collective-permute-start(f32[8,9,16,128]{3,2,1,0:T(8,128)} %get-tuple-element.23), channel_id=1, source_target_pairs={{0,32},{32,0},{1,33},{33,1},{2,34},{34,2},{3,35},{35,3},{4,36},{36... | collective-permute-start | bytes 1769480 | tf_op jit(solution)/shard_map/ppermute | solution.py:320
  69.0 2.9 %copy-start.4 = (f32[8,32,128]{2,1,0:T(8,128)S(1)}, f32[8,32,128]{2,1,0:T(8,128)}, u32[]{:S(2)}) copy-start(f32[8,32,128]{2,1,0:T(8,128)} %get-tuple-element.20) | copy-start | bytes 393220
  69.1 16.6 %collective-permute-start.5 = (f32[8,9,16,128]{3,2,1,0:T(8,128)S(1)}, f32[8,9,16,128]{3,2,1,0:T(8,128)S(1)}, u32[]{:S(2)}, u32[]{:S(2)}) collective-permute-start(f32[8,9,16,128]{3,2,1,0:T(8,128)S(1)} %add.3), channel_id=1, source_target_pairs={{0,512},{512,0},{1,513},{513,1},{2,514},{514,2},{3,515},{515,3},{4... | collective-permute-start | bytes 1769480 | tf_op jit(solution)/shard_map/ppermute | solution.py:321
  85.6 31.3 %all-to-all-start.3 = ((f32[16,32,128]{2,1,0:T(8,128)}), f32[16,32,128]{2,1,0:T(8,128)S(1)}, u32[]{:S(2)}, u32[]{:S(2)}) async-start(f32[16,32,128]{2,1,0:T(8,128)} %shard_map.98), calls=%async_computation.3 | async-start | bytes 524288 | tf_op jit(solution)/shard_map/all_to_all | solution.py:232
  104.0 24.5 %collective-permute-start.7 = (f32[8,3,16,128]{3,2,1,0:T(8,128)S(1)}, f32[8,3,16,128]{3,2,1,0:T(8,128)S(1)}, u32[]{:S(2)}, u32[]{:S(2)}) collective-permute-start(f32[8,3,16,128]{3,2,1,0:T(8,128)S(1)} %get-tuple-element.27), channel_id=1, source_target_pairs={{0,1},{1,0},{2,3},{3,2},{4,5},{5,4},{6,7},{7,6},{8,9},{9,8},{10,11... | collective-permute-start | bytes 589832 | tf_op jit(solution)/shard_map/ppermute | solution.py:334
  108.1 20.5 %collective-permute-start.8 = (f32[8,3,16,128]{3,2,1,0:T(8,128)S(1)}, f32[8,3,16,128]{3,2,1,0:T(8,128)S(1)}, u32[]{:S(2)}, u32[]{:S(2)}) collective-permute-start(f32[8,3,16,128]{3,2,1,0:T(8,128)S(1)} %get-tuple-element.28), channel_id=1, source_target_pairs={{1,2},{2,1},{3,4},{4,3},{5,6},{6,5},{7,8},{8,7},{9,10},{10,9},{11,... | collective-permute-start | bytes 589832 | tf_op jit(solution)/shard_map/ppermute | solution.py:335
  117.6 16.3 %all-to-all-start.4 = ((f32[8,32,128]{2,1,0:T(8,128)}), f32[8,32,128]{2,1,0:T(8,128)S(1)}, u32[]{:S(2)}, u32[]{:S(2)}) async-start(f32[8,32,128]{2,1,0:T(8,128)} %shard_map.100), calls=%async_computation.4 | async-start | bytes 262144 | tf_op jit(solution)/shard_map/all_to_all | solution.py:232

commit v5 on v3

--- a/solution.py
+++ b/solution.py
@@ -10,12 +10,11 @@
 PLANE = ("xl", "y")
 ANGLE = ("xl", "y", "c")
 SCAN = ("z", "xh")
-ROW = ("xl", "c", "xh")
+ROW = ("c", "xh")
 ANY = pl.BlockSpec(memory_space=pl.ANY)
 VMEM = pl.BlockSpec(memory_space=pltpu.VMEM)
 SMEM = pl.BlockSpec(memory_space=pltpu.SMEM)
 HBM = pl.BlockSpec(memory_space=pltpu.HBM)
-URGENT = pl.CostEstimate(flops=50_000_000_000, bytes_accessed=1_000_000, transcendentals=0)
 SMALL = pltpu.CompilerParams(vmem_limit_bytes=8 * 1024 * 1024)
 
 
@@ -86,19 +85,17 @@
 
 def gradient_kernel(
     info, table, probe, measured, own_mine, own_theirs, rim_mine, rim_theirs,
-    keep_near, keep_far, send_near, send_far, probe_sums,
+    keep, send, probe_sums,
     region, grown, sums, table_here, probe_here, measured_here, arrived, left_sem,
 ):
     slots, size = measured.shape[0], measured.shape[1]
     groups = region.shape[0]
     layers = groups // 3
     half = size // 2
-    rows = keep_near.shape[0]
+    angles = 2 * keep.shape[0]
     core = info[0]
     other = 1 - core
-    near = info[1] * rows
-    far = rows - near
-    place = 2
+    place = 1
     copies = []
 
     def fetch(source, target):
@@ -128,7 +125,7 @@
     folded = jnp.where(rim, lane, lane - half)
     tops = [info[place + p] for p in range(slots)]
     later = [folded < tops[p] for p in range(slots)]
-    weights = [jnp.where(p < info[place + 2 * slots + layers], 4.0 * 0.5 / (4 * rows), 0.0) for p in range(slots)]
+    weights = [jnp.where(p < info[place + 2 * slots + layers], 4.0 * 0.5 / angles, 0.0) for p in range(slots)]
     starts = [
         [info[place + slots + p] + info[place + 2 * slots + k] for k in range(layers)] for p in range(slots)
     ]
@@ -176,10 +173,8 @@
 
     leave(sums, probe_sums)
     for g in range(groups):
-        leave(grown.at[g, pl.ds(near, rows), core], keep_near.at[:, g])
-        leave(grown.at[g, pl.ds(far, rows), core], keep_far.at[:, g])
-        leave(grown.at[g, pl.ds(near, rows), other], send_near.at[:, g])
-        leave(grown.at[g, pl.ds(far, rows), other], send_far.at[:, g])
+        leave(grown.at[g, :, core], keep.at[:, g])
+        leave(grown.at[g, :, other], send.at[:, g])
     for copy in copies:
         copy.start()
     for copy in copies:
@@ -199,11 +194,11 @@
         many[q] = total
 
 
-def share_kernel(info, kept, swapped, crossed, own, to_paired, to_crossed):
+def share_kernel(info, kept, swapped, own, to_paired, to_crossed):
     layers = own.shape[1]
     odd = info[0] == 1
     for q in range(own.shape[0]):
-        total = kept[q] + swapped[q] + crossed[q]
+        total = kept[q] + swapped[q]
         before, after = total[layers : 2 * layers], total[2 * layers :]
         own[q] = total[:layers]
         to_paired[q] = jnp.where(odd, before, after)
@@ -239,7 +234,6 @@
     slots = row_offsets.shape[2]
     angles = lax.axis_size(ANGLE)
     plane = angles // 2
-    rows = plane // 2
     scans = lax.axis_size(SCAN)
     pairs = [(i, i ^ 1) for i in range(scans)]
     others = [(i, i + 1 if i % 2 else i - 1) for i in range(1, scans - 1)]
@@ -251,7 +245,6 @@
     info = jnp.concatenate(
         [
             core.astype(jnp.int32)[None],
-            lax.axis_index("xl").astype(jnp.int32)[None],
             row_offsets.reshape(slots),
             column_starts.reshape(slots),
             slice_shifts.reshape(layers),
@@ -283,15 +276,15 @@
     rim_mine = exchanged(rim_many, PLANE)
     rim_theirs = lax.ppermute(rim_mine, "c", swap)
 
-    share = jax.ShapeDtypeStruct((rows, groups, width, size), jnp.float32)
+    share = jax.ShapeDtypeStruct((plane, groups, width, size), jnp.float32)
     depth = lax.axis_size("z")
-    piece = jax.ShapeDtypeStruct((rows, 2 * size // rows, size), jnp.float32)
+    piece = jax.ShapeDtypeStruct((plane, 2 * size // plane, size), jnp.float32)
     table = jnp.asarray(tables(size))
-    keep_near, keep_far, send_near, send_far, probe_sums = pl.pallas_call(
+    keep, send, probe_sums = pl.pallas_call(
         gradient_kernel,
-        out_shape=(share, share, share, share, piece),
+        out_shape=(share, *[pltpu.HBM(x.shape, x.dtype) for x in (share, piece)]),
         in_specs=[SMEM] + [HBM] * 3 + [ANY] * 4,
-        out_specs=[HBM] * 5,
+        out_specs=[HBM] * 3,
         scratch_shapes=[
             pltpu.VMEM((groups, plane, 2, width, size), jnp.float32),
             pltpu.VMEM((groups, plane, 2, width, size), jnp.float32),
@@ -300,10 +293,10 @@
             pltpu.VMEM(probe.shape, jnp.float32),
             pltpu.VMEM((slots, size, size), jnp.float32),
             pltpu.SemaphoreType.DMA((2 * groups + 3,)),
-            pltpu.SemaphoreType.DMA((4 * groups + 1,)),
+            pltpu.SemaphoreType.DMA((2 * groups + 1,)),
         ],
-        compiler_params=pltpu.CompilerParams(vmem_limit_bytes=52 * 1024 * 1024),
-    )(info, table, probe, intensities[0, 0], own_mine, own_theirs, rim_mine, rim_theirs)
+        compiler_params=pltpu.CompilerParams(vmem_limit_bytes=32 * 1024 * 1024),
+    )(info, *[pltpu.with_memory_space_constraint(x, pltpu.HBM) for x in (table, probe, intensities[0, 0])], own_mine, own_theirs, rim_mine, rim_theirs)
 
     def probe_total(parts, count):
         return pl.pallas_call(
@@ -312,30 +305,26 @@
             in_specs=[VMEM],
             out_specs=VMEM,
             compiler_params=SMALL,
-            cost_estimate=URGENT,
         )(parts)
 
-    parts = exchanged(probe_sums, "y")
+    parts = exchanged(probe_sums, PLANE)
+    swapped = lax.ppermute(send, "c", swap)
     parts = exchanged(probe_total(parts, depth), "z")
-    parts = exchanged(probe_total(parts, lax.axis_size(ROW)), ROW)
-
-    part_far = keep_far + lax.ppermute(send_far, "c", swap)
-    swapped = lax.ppermute(send_near, "c", swap)
-    crossed = lax.ppermute(part_far, "xl", swap)
-    band_share = jax.ShapeDtypeStruct((rows, *tile), jnp.float32)
+    band_share = jax.ShapeDtypeStruct((plane, *tile), jnp.float32)
     own_share, to_paired, to_crossed = pl.pallas_call(
         share_kernel,
         out_shape=(band_share, band_share, band_share),
-        in_specs=[SMEM] + [VMEM] * 3,
+        in_specs=[SMEM] + [VMEM] * 2,
         out_specs=[VMEM] * 3,
         compiler_params=SMALL,
-    )(odd, keep_near, swapped, crossed)
+    )(odd, keep, swapped)
+    parts = exchanged(probe_total(parts, lax.axis_size(ROW)), ROW)
     from_paired = lax.ppermute(to_paired, SCAN, pairs)
     from_crossed = lax.ppermute(to_crossed, SCAN, others)
     extra = piece.shape[1] // width
     joined = pl.pallas_call(
         join_kernel,
-        out_shape=jax.ShapeDtypeStruct((rows, layers + extra, width, size), jnp.float32),
+        out_shape=jax.ShapeDtypeStruct((plane, layers + extra, width, size), jnp.float32),
         in_specs=[VMEM] * 4,
         out_specs=VMEM,
         compiler_params=SMALL,
@@ -346,7 +335,7 @@
         in_specs=[VMEM],
         out_specs=[VMEM] * 2,
         compiler_params=SMALL,
-    )(exchanged(joined, "y"))
+    )(exchanged(joined, PLANE))
     return (jnp.swapaxes(object_gradient, 2, 3), probe_gradient.reshape(probe.shape))
 
 

time: 156 us -> 142 us (0.910)
  the two profiles are of different devices: /device:TPU:1 before, /device:TPU:14 now
where the time goes in v5:
time: 142 us; the launch traced here: 141 us
  blocking collectives  67.1 us (47%)
  starting transfers between devices  54 us (38%)
  Pallas kernels  10.6 us (7%)
  waiting for transfers between devices  6.84 us (5%)
  between operations  1.44 us (1%)
    all_to_all x4, blocking collectives, exchanged(): return lax.all_to_all(array, axes, 0, 0, tiled=True)  67.1 us
    all_to_all x2, starting transfers between devices, exchanged(): return lax.all_to_all(array, axes, 0, 0, tiled=True)  26.7 us
    pallas_call x1, Pallas kernels, local(): pl.pallas_call(gradient_kernel, out_shape=(share, *[pltpu.HBM(x.shape, x....  7.36 us
    ppermute x1, starting transfers between devices, local(): paired = lax.ppermute(packed, SCAN, pairs)  6.85 us
    ppermute x1, starting transfers between devices, local(): from_crossed = lax.ppermute(to_crossed, SCAN, others)  5.13 us
    ppermute x1, starting transfers between devices, local(): crossed = lax.ppermute(packed, SCAN, others)  5.11 us
    all_to_all x2, waiting for transfers between devices, exchanged(): return lax.all_to_all(array, axes, 0, 0, tiled=True)  4.4 us
    ppermute x1, starting transfers between devices, local(): from_paired = lax.ppermute(to_paired, SCAN, pairs)  3.56 us
  transfers between devices with their start and end apart: 9, of which 3 were waited for; matrix products, arithmetic and copies ran while one was open for 0% of the time, Pallas kernels for 1%

profile of v5, /device:TPU:14, one launch (start us, length us, event | category | flops | bytes accessed | tf_op | source)
XLA Modules:
  0.0 140.9 jit_solution(5301157027654665878)
XLA Ops:
  0.6 0.0 copy-start
  0.6 0.8 copy-done
  1.4 0.8 shard_map.95
  2.3 8.5 %all-to-all-start = ((f32[16,3,16,128]{3,2,1,0:T(8,128)}), f32[16,3,16,128]{3,2,1,0:T(8,128)S(1)}, u32[]{:S(2)}, u32[]{:S(2)}) async-start(f32[16,3,16,128]{3,2,1,0:T(8,128)} %get-tuple-element.12), calls=%async_computation | async-start | bytes 786432 | tf_op jit(solution)/shard_map/all_to_all | solution.py:227
  10.7 5.1 %collective-permute-start.2 = (f32[3,16,128]{2,1,0:T(8,128)S(1)}, f32[3,16,128]{2,1,0:T(8,128)S(1)}, u32[]{:S(2)}, u32[]{:S(2)}) collective-permute-start(f32[3,16,128]{2,1,0:T(8,128)S(1)} %get-tuple-element.13), channel_id=1, source_target_pairs={{1,2},{2,1},{3,4},{4,3},{5,6},{6,5},{7,8},{8,7},{9,10},{10,9},{11,... | collective-permute-start | bytes 73736 | tf_op jit(solution)/shard_map/ppermute | solution.py:267
  15.9 6.9 %collective-permute-start.1 = (f32[3,16,128]{2,1,0:T(8,128)S(1)}, f32[3,16,128]{2,1,0:T(8,128)S(1)}, u32[]{:S(2)}, u32[]{:S(2)}) collective-permute-start(f32[3,16,128]{2,1,0:T(8,128)S(1)} %get-tuple-element.13), channel_id=1, source_target_pairs={{0,1},{1,0},{2,3},{3,2},{4,5},{5,4},{6,7},{7,6},{8,9},{9,8},{10,11... | collective-permute-start | bytes 73736 | tf_op jit(solution)/shard_map/ppermute | solution.py:266
  22.7 0.0 collective-permute-done.2.crossed
  22.7 1.9 %collective-permute-done.1.paired = f32[3,16,128]{2,1,0:T(8,128)S(1)} collective-permute-done((f32[3,16,128]{2,1,0:T(8,128)S(1)}, f32[3,16,128]{2,1,0:T(8,128)S(1)}, u32[]{:S(2)}, u32[]{:S(2)}) %collective-permute-start.1) | collective-permute-done | bytes 24608 | tf_op jit(solution)/shard_map/ppermute | solution.py:266
  24.6 0.0 all-to-all-done.unused.own_mine
  24.6 0.1 shard_map.96
  24.7 25.6 %all_to_all.30.rim_mine = f32[16,6,16,128]{3,2,1,0:T(8,128)S(1)} all-to-all(f32[16,6,16,128]{3,2,1,0:T(8,128)S(1)} %shard_map.96), channel_id=1, replica_groups=mesh['xl'=2,'y'=8,'c'=2,'z'=16,'xh'=2] {'xl','y'}, dimensions={0} | all-to-all | bytes 1572864 | tf_op jit(solution)/shard_map/all_to_all | solution.py:227
  50.3 1.9 %collective-permute-start.3 = (f32[16,6,16,128]{3,2,1,0:T(8,128)S(1)}, f32[16,6,16,128]{3,2,1,0:T(8,128)S(1)}, u32[]{:S(2)}, u32[]{:S(2)}) collective-permute-start(f32[16,6,16,128]{3,2,1,0:T(8,128)S(1)} %all_to_all.30.rim_mine), channel_id=1, source_target_pairs={{0,32},{32,0},{1,33},{33,1},{2,34},{34,2},{3,35},{35,3},{4,36},{36... | collective-permute-start | bytes 2359304 | tf_op jit(solution)/shard_map/ppermute | solution.py:277
  52.2 2.4 %collective-permute-start = (f32[16,3,16,128]{3,2,1,0:T(8,128)S(1)}, f32[16,3,16,128]{3,2,1,0:T(8,128)S(1)}, u32[]{:S(2)}, u32[]{:S(2)}) collective-permute-start(f32[16,3,16,128]{3,2,1,0:T(8,128)S(1)} %all-to-all-done.unused.own_mine), channel_id=1, source_target_pairs={{0,32},{32,0},{1,33},{33,1},{2,34},{34,2},{3,35},{35,3},{4,36},{36... | collective-permute-start | bytes 1179656 | tf_op jit(solution)/shard_map/ppermute | solution.py:275
  55.3 0.1 concatenate.3.info
  55.4 0.6 collective-permute-done.own_theirs
  55.9 0.0 collective-permute-done.3.rim_theirs
  56.0 7.4 %shard_map.97 = (f32[16,9,16,128]{3,2,1,0:T(8,128)S(1)}, f32[16,9,16,128]{3,2,1,0:T(8,128)}, f32[16,16,128]{2,1,0:T(8,128)}) custom-call(s32[9]{0:T(128)S(1)} %concatenate.3.info, bf16[2,2,2,128,128]{4,3,2,1,0:T(8,128)(2,1)} %constant.10.clone.table, f32[2,128,128]{2,1,0:T(8,128)} %probe.1, f32[2,128,128]{2,1,0:T(8,128)} %bitcast.12, ...), custom_call_target="tpu_custom_call" | custom-call | tf_op jit(solution)/shard_map/pallas_call | solution.py:283
  63.3 2.3 %collective-permute-start.4 = (f32[16,9,16,128]{3,2,1,0:T(8,128)}, f32[16,9,16,128]{3,2,1,0:T(8,128)S(1)}, u32[]{:S(2)}, u32[]{:S(2)}) collective-permute-start(f32[16,9,16,128]{3,2,1,0:T(8,128)} %get-tuple-element.15), channel_id=1, source_target_pairs={{0,32},{32,0},{1,33},{33,1},{2,34},{34,2},{3,35},{35,3},{4,36},{36... | collective-permute-start | bytes 3538952 | tf_op jit(solution)/shard_map/ppermute | solution.py:311
  65.6 12.4 %all_to_all.31.parts = f32[16,16,128]{2,1,0:T(8,128)S(1)} all-to-all(f32[16,16,128]{2,1,0:T(8,128)} %get-tuple-element.19), channel_id=1, replica_groups=mesh['xl'=2,'y'=8,'c'=2,'z'=16,'xh'=2] {'xl','y'}, dimensions={0} | all-to-all | bytes 262144 | tf_op jit(solution)/shard_map/all_to_all | solution.py:227
  78.0 0.7 shard_map.99
  78.7 18.2 %all-to-all-start.3 = ((f32[16,16,128]{2,1,0:T(8,128)}), f32[16,16,128]{2,1,0:T(8,128)S(1)}, u32[]{:S(2)}, u32[]{:S(2)}) async-start(f32[16,16,128]{2,1,0:T(8,128)} %shard_map.99), calls=%async_computation.3 | async-start | bytes 262144 | tf_op jit(solution)/shard_map/all_to_all | solution.py:227
  97.0 0.0 collective-permute-done.4.swapped
  97.0 0.9 shard_map.98
  97.9 3.6 %collective-permute-start.5 = (f32[16,3,16,128]{3,2,1,0:T(8,128)}, f32[16,3,16,128]{3,2,1,0:T(8,128)S(1)}, u32[]{:S(2)}, u32[]{:S(2)}) collective-permute-start(f32[16,3,16,128]{3,2,1,0:T(8,128)} %get-tuple-element.17), channel_id=1, source_target_pairs={{0,1},{1,0},{2,3},{3,2},{4,5},{5,4},{6,7},{7,6},{8,9},{9,8},{10,11... | collective-permute-start | bytes 1179656 | tf_op jit(solution)/shard_map/ppermute | solution.py:322
  101.4 5.1 %collective-permute-start.6 = (f32[16,3,16,128]{3,2,1,0:T(8,128)S(1)}, f32[16,3,16,128]{3,2,1,0:T(8,128)S(1)}, u32[]{:S(2)}, u32[]{:S(2)}) collective-permute-start(f32[16,3,16,128]{3,2,1,0:T(8,128)S(1)} %get-tuple-element.18), channel_id=1, source_target_pairs={{1,2},{2,1},{3,4},{4,3},{5,6},{6,5},{7,8},{8,7},{9,10},{10,9},{11,... | collective-permute-start | bytes 1179656 | tf_op jit(solution)/shard_map/ppermute | solution.py:323
  106.6 4.4 %all-to-all-done.3.parts = f32[16,16,128]{2,1,0:T(8,128)S(1)} async-done(((f32[16,16,128]{2,1,0:T(8,128)}), f32[16,16,128]{2,1,0:T(8,128)S(1)}, u32[]{:S(2)}, u32[]{:S(2)}) %all-to-all-start.3) | async-done | bytes 131104 | tf_op jit(solution)/shard_map/all_to_all | solution.py:227
  111.0 8.6 %all_to_all.32.parts = f32[4,16,128]{2,1,0:T(8,128)S(1)} all-to-all(f32[4,16,128]{2,1,0:T(8,128)S(1)} %shard_map.100), channel_id=1, replica_groups=mesh['xl'=2,'y'=8,'c'=2,'z'=16,'xh'=2] {'c','xh'}, dimensions={0} | all-to-all | bytes 65536 | tf_op jit(solution)/shard_map/all_to_all | solution.py:227
  119.6 0.0 collective-permute-done.5.from_paired
  119.6 0.0 collective-permute-done.6.from_crossed
  119.6 0.1 shard_map.101
  119.7 20.5 %all_to_all.33.shares = f32[16,4,16,128]{3,2,1,0:T(8,128)S(1)} all-to-all(f32[16,4,16,128]{3,2,1,0:T(8,128)S(1)} %shard_map.101), channel_id=1, replica_groups=mesh['xl'=2,'y'=8,'c'=2,'z'=16,'xh'=2] {'xl','y'}, dimensions={0} | all-to-all | bytes 1048576 | tf_op jit(solution)/shard_map/all_to_all | solution.py:227
  140.2 0.7 shard_map.102
  (7 shorter events, 0.0 us)
Async XLA Ops:
  0.6 0.8 copy-start
  2.3 22.3 %all-to-all-start = ((f32[16,3,16,128]{3,2,1,0:T(8,128)}), f32[16,3,16,128]{3,2,1,0:T(8,128)S(1)}, u32[]{:S(2)}, u32[]{:S(2)}) async-start(f32[16,3,16,128]{3,2,1,0:T(8,128)} %get-tuple-element.12), calls=%async_computation | async-start | bytes 786432 | tf_op jit(solution)/shard_map/all_to_all | solution.py:227
  10.7 12.0 %collective-permute-start.2 = (f32[3,16,128]{2,1,0:T(8,128)S(1)}, f32[3,16,128]{2,1,0:T(8,128)S(1)}, u32[]{:S(2)}, u32[]{:S(2)}) collective-permute-start(f32[3,16,128]{2,1,0:T(8,128)S(1)} %get-tuple-element.13), channel_id=1, source_target_pairs={{1,2},{2,1},{3,4},{4,3},{5,6},{6,5},{7,8},{8,7},{9,10},{10,9},{11,... | collective-permute-start | bytes 73736 | tf_op jit(solution)/shard_map/ppermute | solution.py:267
  15.9 8.7 %collective-permute-start.1 = (f32[3,16,128]{2,1,0:T(8,128)S(1)}, f32[3,16,128]{2,1,0:T(8,128)S(1)}, u32[]{:S(2)}, u32[]{:S(2)}) collective-permute-start(f32[3,16,128]{2,1,0:T(8,128)S(1)} %get-tuple-element.13), channel_id=1, source_target_pairs={{0,1},{1,0},{2,3},{3,2},{4,5},{5,4},{6,7},{7,6},{8,9},{9,8},{10,11... | collective-permute-start | bytes 73736 | tf_op jit(solution)/shard_map/ppermute | solution.py:266
  24.6 30.7 %copy-start.1 = (s32[1,1,2]{2,1,0:T(1,128)S(1)}, s32[1,1,2]{2,1,0:T(1,128)}, u32[]{:S(2)}) copy-start(s32[1,1,2]{2,1,0:T(1,128)} %param.11) | copy-start | bytes 28
  24.6 30.7 %copy-start.2 = (s32[1,1,2]{2,1,0:T(1,128)S(1)}, s32[1,1,2]{2,1,0:T(1,128)}, u32[]{:S(2)}) copy-start(s32[1,1,2]{2,1,0:T(1,128)} %param.12) | copy-start | bytes 28
  24.6 30.7 %copy-start.3 = (s32[1,3]{1,0:T(1,128)S(1)}, s32[1,3]{1,0:T(1,128)}, u32[]{:S(2)}) copy-start(s32[1,3]{1,0:T(1,128)} %param.13) | copy-start | bytes 40
  50.3 5.7 %collective-permute-start.3 = (f32[16,6,16,128]{3,2,1,0:T(8,128)S(1)}, f32[16,6,16,128]{3,2,1,0:T(8,128)S(1)}, u32[]{:S(2)}, u32[]{:S(2)}) collective-permute-start(f32[16,6,16,128]{3,2,1,0:T(8,128)S(1)} %all_to_all.30.rim_mine), channel_id=1, source_target_pairs={{0,32},{32,0},{1,33},{33,1},{2,34},{34,2},{3,35},{35,3},{4,36},{36... | collective-permute-start | bytes 2359304 | tf_op jit(solution)/shard_map/ppermute | solution.py:277
  52.2 3.7 %collective-permute-start = (f32[16,3,16,128]{3,2,1,0:T(8,128)S(1)}, f32[16,3,16,128]{3,2,1,0:T(8,128)S(1)}, u32[]{:S(2)}, u32[]{:S(2)}) collective-permute-start(f32[16,3,16,128]{3,2,1,0:T(8,128)S(1)} %all-to-all-done.unused.own_mine), channel_id=1, source_target_pairs={{0,32},{32,0},{1,33},{33,1},{2,34},{34,2},{3,35},{35,3},{4,36},{36... | collective-permute-start | bytes 1179656 | tf_op jit(solution)/shard_map/ppermute | solution.py:275
  63.3 33.7 %collective-permute-start.4 = (f32[16,9,16,128]{3,2,1,0:T(8,128)}, f32[16,9,16,128]{3,2,1,0:T(8,128)S(1)}, u32[]{:S(2)}, u32[]{:S(2)}) collective-permute-start(f32[16,9,16,128]{3,2,1,0:T(8,128)} %get-tuple-element.15), channel_id=1, source_target_pairs={{0,32},{32,0},{1,33},{33,1},{2,34},{34,2},{3,35},{35,3},{4,36},{36... | collective-permute-start | bytes 3538952 | tf_op jit(solution)/shard_map/ppermute | solution.py:311
  78.7 32.2 %all-to-all-start.3 = ((f32[16,16,128]{2,1,0:T(8,128)}), f32[16,16,128]{2,1,0:T(8,128)S(1)}, u32[]{:S(2)}, u32[]{:S(2)}) async-start(f32[16,16,128]{2,1,0:T(8,128)} %shard_map.99), calls=%async_computation.3 | async-start | bytes 262144 | tf_op jit(solution)/shard_map/all_to_all | solution.py:227
  97.9 21.7 %collective-permute-start.5 = (f32[16,3,16,128]{3,2,1,0:T(8,128)}, f32[16,3,16,128]{3,2,1,0:T(8,128)S(1)}, u32[]{:S(2)}, u32[]{:S(2)}) collective-permute-start(f32[16,3,16,128]{3,2,1,0:T(8,128)} %get-tuple-element.17), channel_id=1, source_target_pairs={{0,1},{1,0},{2,3},{3,2},{4,5},{5,4},{6,7},{7,6},{8,9},{9,8},{10,11... | collective-permute-start | bytes 1179656 | tf_op jit(solution)/shard_map/ppermute | solution.py:322
  101.4 18.2 %collective-permute-start.6 = (f32[16,3,16,128]{3,2,1,0:T(8,128)S(1)}, f32[16,3,16,128]{3,2,1,0:T(8,128)S(1)}, u32[]{:S(2)}, u32[]{:S(2)}) collective-permute-start(f32[16,3,16,128]{3,2,1,0:T(8,128)S(1)} %get-tuple-element.18), channel_id=1, source_target_pairs={{1,2},{2,1},{3,4},{4,3},{5,6},{6,5},{7,8},{8,7},{9,10},{10,9},{11,... | collective-permute-start | bytes 1179656 | tf_op jit(solution)/shard_map/ppermute | solution.py:323

commit v6 on v5

--- a/solution.py
+++ b/solution.py
@@ -274,6 +274,7 @@
     )(odd, paired, crossed, own_mine)
     own_theirs = lax.ppermute(own_mine, "c", swap)
     rim_mine = exchanged(rim_many, PLANE)
+    rim_mine, own_theirs = lax.optimization_barrier((rim_mine, own_theirs))
     rim_theirs = lax.ppermute(rim_mine, "c", swap)
 
     share = jax.ShapeDtypeStruct((plane, groups, width, size), jnp.float32)

time: 142 us -> 141 us (level)
  blocking collectives: 67.1 us -> 42.4 us
  waiting for transfers between devices: 6.84 us -> 22.2 us
  starting transfers between devices: 54 us -> 62.3 us
    all_to_all x4 -> x3, blocking collectives: 67.1 us -> 42.4 us  [exchanged(): return lax.all_to_all(array, axes, 0, 0, tiled=True)]
    all_to_all x2 -> x3, waiting for transfers between devices: 4.4 us -> 17.1 us  [exchanged(): return lax.all_to_all(array, axes, 0, 0, tiled=True)]
    all_to_all x2 -> x3, starting transfers between devices: 26.7 us -> 35.8 us  [exchanged(): return lax.all_to_all(array, axes, 0, 0, tiled=True)]
    ppermute x1, waiting for transfers between devices: 0.01 us -> 1.49 us  [local(): rim_theirs = lax.ppermute(rim_mine, 'c', swap)]
  transfers between devices with their start and end apart: 9 -> 10, of which waited for: 3 -> 5; matrix products, arithmetic and copies ran while one was open for 0% -> 0% of each run, Pallas kernels for 1% -> 1%
where the time goes in v6:
time: 141 us
  starting transfers between devices  62.3 us (44%)
  blocking collectives  42.4 us (30%)
  waiting for transfers between devices  22.2 us (16%)
  Pallas kernels  11.5 us (8%)
  between operations  1.43 us (1%)
    all_to_all x3, blocking collectives, exchanged(): return lax.all_to_all(array, axes, 0, 0, tiled=True)  42.4 us
    all_to_all x3, starting transfers between devices, exchanged(): return lax.all_to_all(array, axes, 0, 0, tiled=True)  35.8 us
    all_to_all x3, waiting for transfers between devices, exchanged(): return lax.all_to_all(array, axes, 0, 0, tiled=True)  17.1 us
    pallas_call x1, Pallas kernels, local(): pl.pallas_call(gradient_kernel, out_shape=(share, *[pltpu.HBM(x.shape, x....  7.34 us
    ppermute x1, starting transfers between devices, local(): paired = lax.ppermute(packed, SCAN, pairs)  6.85 us
    ppermute x1, starting transfers between devices, local(): crossed = lax.ppermute(packed, SCAN, others)  5.11 us
    ppermute x1, starting transfers between devices, local(): from_crossed = lax.ppermute(to_crossed, SCAN, others)  5.11 us
    ppermute x1, starting transfers between devices, local(): from_paired = lax.ppermute(to_paired, SCAN, pairs)  3.58 us
  transfers between devices with their start and end apart: 10, of which 5 were waited for; matrix products, arithmetic and copies ran while one was open for 0% of the time, Pallas kernels for 1%

profile of v6, /device:TPU:14, one launch (start us, length us, event | category | flops | bytes accessed | tf_op | source)
XLA Modules:
  0.0 140.7 jit_solution(1913901114227035786)
XLA Ops:
  0.6 0.8 copy-done
  1.4 0.8 shard_map.95
  2.3 8.5 %all-to-all-start = ((f32[16,3,16,128]{3,2,1,0:T(8,128)}), f32[16,3,16,128]{3,2,1,0:T(8,128)S(1)}, u32[]{:S(2)}, u32[]{:S(2)}) async-start(f32[16,3,16,128]{3,2,1,0:T(8,128)} %get-tuple-element.14), calls=%async_computation | async-start | bytes 786432 | tf_op jit(solution)/shard_map/all_to_all | solution.py:227
  10.7 5.1 %collective-permute-start.1 = (f32[3,16,128]{2,1,0:T(8,128)S(1)}, f32[3,16,128]{2,1,0:T(8,128)S(1)}, u32[]{:S(2)}, u32[]{:S(2)}) collective-permute-start(f32[3,16,128]{2,1,0:T(8,128)S(1)} %get-tuple-element.15), channel_id=1, source_target_pairs={{1,2},{2,1},{3,4},{4,3},{5,6},{6,5},{7,8},{8,7},{9,10},{10,9},{11,... | collective-permute-start | bytes 73736 | tf_op jit(solution)/shard_map/ppermute | solution.py:267
  15.9 6.9 %collective-permute-start = (f32[3,16,128]{2,1,0:T(8,128)S(1)}, f32[3,16,128]{2,1,0:T(8,128)S(1)}, u32[]{:S(2)}, u32[]{:S(2)}) collective-permute-start(f32[3,16,128]{2,1,0:T(8,128)S(1)} %get-tuple-element.15), channel_id=1, source_target_pairs={{0,1},{1,0},{2,3},{3,2},{4,5},{5,4},{6,7},{7,6},{8,9},{9,8},{10,11... | collective-permute-start | bytes 73736 | tf_op jit(solution)/shard_map/ppermute | solution.py:266
  22.7 0.0 collective-permute-done.1.crossed
  22.7 1.9 %collective-permute-done.paired = f32[3,16,128]{2,1,0:T(8,128)S(1)} collective-permute-done((f32[3,16,128]{2,1,0:T(8,128)S(1)}, f32[3,16,128]{2,1,0:T(8,128)S(1)}, u32[]{:S(2)}, u32[]{:S(2)}) %collective-permute-start) | collective-permute-done | bytes 24608 | tf_op jit(solution)/shard_map/ppermute | solution.py:266
  24.6 0.0 all-to-all-done.unused.own_mine
  24.6 1.0 shard_map.96
  25.6 9.1 %all-to-all-start.1 = ((f32[16,6,16,128]{3,2,1,0:T(8,128)}), f32[16,6,16,128]{3,2,1,0:T(8,128)S(1)}, u32[]{:S(2)}, u32[]{:S(2)}) async-start(f32[16,6,16,128]{3,2,1,0:T(8,128)} %shard_map.96), calls=%async_computation.1 | async-start | bytes 1572864 | tf_op jit(solution)/shard_map/all_to_all | solution.py:227
  34.7 1.9 %collective-permute-start.2 = (f32[16,3,16,128]{3,2,1,0:T(8,128)S(1)}, f32[16,3,16,128]{3,2,1,0:T(8,128)S(1)}, u32[]{:S(2)}, u32[]{:S(2)}) collective-permute-start(f32[16,3,16,128]{3,2,1,0:T(8,128)S(1)} %all-to-all-done.unused.own_mine), channel_id=1, source_target_pairs={{0,32},{32,0},{1,33},{33,1},{2,34},{34,2},{3,35},{35,3},{4,36},{36... | collective-permute-start | bytes 1179656 | tf_op jit(solution)/shard_map/ppermute | solution.py:275
  36.6 1.7 %collective-permute-done.2.own_theirs = f32[16,3,16,128]{3,2,1,0:T(8,128)S(1)} collective-permute-done((f32[16,3,16,128]{3,2,1,0:T(8,128)S(1)}, f32[16,3,16,128]{3,2,1,0:T(8,128)S(1)}, u32[]{:S(2)}, u32[]{:S(2)}) %collective-permute-start.2) | collective-permute-done | bytes 393248 | tf_op jit(solution)/shard_map/ppermute | solution.py:275
  38.3 12.6 %all-to-all-done.1.rim_mine = f32[16,6,16,128]{3,2,1,0:T(8,128)S(1)} async-done(((f32[16,6,16,128]{3,2,1,0:T(8,128)}), f32[16,6,16,128]{3,2,1,0:T(8,128)S(1)}, u32[]{:S(2)}, u32[]{:S(2)}) %all-to-all-start.1) | async-done | bytes 786464 | tf_op jit(solution)/shard_map/all_to_all | solution.py:227
  50.8 1.9 %collective-permute-start.3 = (f32[16,6,16,128]{3,2,1,0:T(8,128)S(1)}, f32[16,6,16,128]{3,2,1,0:T(8,128)S(1)}, u32[]{:S(2)}, u32[]{:S(2)}) collective-permute-start(f32[16,6,16,128]{3,2,1,0:T(8,128)S(1)} %all-to-all-done.1.rim_mine), channel_id=1, source_target_pairs={{0,32},{32,0},{1,33},{33,1},{2,34},{34,2},{3,35},{35,3},{4,36},{36... | collective-permute-start | bytes 2359304 | tf_op jit(solution)/shard_map/ppermute | solution.py:278
  53.4 0.1 concatenate.3.info
  53.5 1.5 %collective-permute-done.3.rim_theirs = f32[16,6,16,128]{3,2,1,0:T(8,128)S(1)} collective-permute-done((f32[16,6,16,128]{3,2,1,0:T(8,128)S(1)}, f32[16,6,16,128]{3,2,1,0:T(8,128)S(1)}, u32[]{:S(2)}, u32[]{:S(2)}) %collective-permute-start.3) | collective-permute-done | bytes 786464 | tf_op jit(solution)/shard_map/ppermute | solution.py:278
  55.0 7.3 %shard_map.97 = (f32[16,9,16,128]{3,2,1,0:T(8,128)S(1)}, f32[16,9,16,128]{3,2,1,0:T(8,128)}, f32[16,16,128]{2,1,0:T(8,128)}) custom-call(s32[9]{0:T(128)S(1)} %concatenate.3.info, bf16[2,2,2,128,128]{4,3,2,1,0:T(8,128)(2,1)} %constant.10.clone.table, f32[2,128,128]{2,1,0:T(8,128)} %probe.1, f32[2,128,128]{2,1,0:T(8,128)} %bitcast.12, ...), custom_call_target="tpu_custom_call" | custom-call | tf_op jit(solution)/shard_map/pallas_call | solution.py:284
  62.4 2.1 %collective-permute-start.4 = (f32[16,9,16,128]{3,2,1,0:T(8,128)}, f32[16,9,16,128]{3,2,1,0:T(8,128)S(1)}, u32[]{:S(2)}, u32[]{:S(2)}) collective-permute-start(f32[16,9,16,128]{3,2,1,0:T(8,128)} %get-tuple-element.19), channel_id=1, source_target_pairs={{0,32},{32,0},{1,33},{33,1},{2,34},{34,2},{3,35},{35,3},{4,36},{36... | collective-permute-start | bytes 3538952 | tf_op jit(solution)/shard_map/ppermute | solution.py:312
  64.4 13.2 %all_to_all.30.parts = f32[16,16,128]{2,1,0:T(8,128)S(1)} all-to-all(f32[16,16,128]{2,1,0:T(8,128)} %get-tuple-element.23), channel_id=1, replica_groups=mesh['xl'=2,'y'=8,'c'=2,'z'=16,'xh'=2] {'xl','y'}, dimensions={0} | all-to-all | bytes 262144 | tf_op jit(solution)/shard_map/all_to_all | solution.py:227
  77.7 0.7 shard_map.99
  78.3 18.2 %all-to-all-start.3 = ((f32[16,16,128]{2,1,0:T(8,128)}), f32[16,16,128]{2,1,0:T(8,128)S(1)}, u32[]{:S(2)}, u32[]{:S(2)}) async-start(f32[16,16,128]{2,1,0:T(8,128)} %shard_map.99), calls=%async_computation.3 | async-start | bytes 262144 | tf_op jit(solution)/shard_map/all_to_all | solution.py:227
  96.6 0.0 collective-permute-done.4.swapped
  96.6 0.9 shard_map.98
  97.5 3.6 %collective-permute-start.5 = (f32[16,3,16,128]{3,2,1,0:T(8,128)}, f32[16,3,16,128]{3,2,1,0:T(8,128)S(1)}, u32[]{:S(2)}, u32[]{:S(2)}) collective-permute-start(f32[16,3,16,128]{3,2,1,0:T(8,128)} %get-tuple-element.21), channel_id=1, source_target_pairs={{0,1},{1,0},{2,3},{3,2},{4,5},{5,4},{6,7},{7,6},{8,9},{9,8},{10,11... | collective-permute-start | bytes 1179656 | tf_op jit(solution)/shard_map/ppermute | solution.py:323
  101.0 5.1 %collective-permute-start.6 = (f32[16,3,16,128]{3,2,1,0:T(8,128)S(1)}, f32[16,3,16,128]{3,2,1,0:T(8,128)S(1)}, u32[]{:S(2)}, u32[]{:S(2)}) collective-permute-start(f32[16,3,16,128]{3,2,1,0:T(8,128)S(1)} %get-tuple-element.22), channel_id=1, source_target_pairs={{1,2},{2,1},{3,4},{4,3},{5,6},{6,5},{7,8},{8,7},{9,10},{10,9},{11,... | collective-permute-start | bytes 1179656 | tf_op jit(solution)/shard_map/ppermute | solution.py:324
  106.2 4.5 %all-to-all-done.3.parts = f32[16,16,128]{2,1,0:T(8,128)S(1)} async-done(((f32[16,16,128]{2,1,0:T(8,128)}), f32[16,16,128]{2,1,0:T(8,128)S(1)}, u32[]{:S(2)}, u32[]{:S(2)}) %all-to-all-start.3) | async-done | bytes 131104 | tf_op jit(solution)/shard_map/all_to_all | solution.py:227
  110.7 9.1 %all_to_all.31.parts = f32[4,16,128]{2,1,0:T(8,128)S(1)} all-to-all(f32[4,16,128]{2,1,0:T(8,128)S(1)} %shard_map.100), channel_id=1, replica_groups=mesh['xl'=2,'y'=8,'c'=2,'z'=16,'xh'=2] {'c','xh'}, dimensions={0} | all-to-all | bytes 65536 | tf_op jit(solution)/shard_map/all_to_all | solution.py:227
  119.8 0.0 collective-permute-done.5.from_paired
  119.8 0.0 collective-permute-done.6.from_crossed
  119.8 0.1 shard_map.101
  119.9 20.1 %all_to_all.32.shares = f32[16,4,16,128]{3,2,1,0:T(8,128)S(1)} all-to-all(f32[16,4,16,128]{3,2,1,0:T(8,128)S(1)} %shard_map.101), channel_id=1, replica_groups=mesh['xl'=2,'y'=8,'c'=2,'z'=16,'xh'=2] {'xl','y'}, dimensions={0} | all-to-all | bytes 1048576 | tf_op jit(solution)/shard_map/all_to_all | solution.py:227
  139.9 0.7 shard_map.102
  (8 shorter events, 0.0 us)
Async XLA Ops:
  0.6 0.8 copy-start
  2.3 22.3 %all-to-all-start = ((f32[16,3,16,128]{3,2,1,0:T(8,128)}), f32[16,3,16,128]{3,2,1,0:T(8,128)S(1)}, u32[]{:S(2)}, u32[]{:S(2)}) async-start(f32[16,3,16,128]{3,2,1,0:T(8,128)} %get-tuple-element.14), calls=%async_computation | async-start | bytes 786432 | tf_op jit(solution)/shard_map/all_to_all | solution.py:227
  10.7 12.0 %collective-permute-start.1 = (f32[3,16,128]{2,1,0:T(8,128)S(1)}, f32[3,16,128]{2,1,0:T(8,128)S(1)}, u32[]{:S(2)}, u32[]{:S(2)}) collective-permute-start(f32[3,16,128]{2,1,0:T(8,128)S(1)} %get-tuple-element.15), channel_id=1, source_target_pairs={{1,2},{2,1},{3,4},{4,3},{5,6},{6,5},{7,8},{8,7},{9,10},{10,9},{11,... | collective-permute-start | bytes 73736 | tf_op jit(solution)/shard_map/ppermute | solution.py:267
  15.9 8.7 %collective-permute-start = (f32[3,16,128]{2,1,0:T(8,128)S(1)}, f32[3,16,128]{2,1,0:T(8,128)S(1)}, u32[]{:S(2)}, u32[]{:S(2)}) collective-permute-start(f32[3,16,128]{2,1,0:T(8,128)S(1)} %get-tuple-element.15), channel_id=1, source_target_pairs={{0,1},{1,0},{2,3},{3,2},{4,5},{5,4},{6,7},{7,6},{8,9},{9,8},{10,11... | collective-permute-start | bytes 73736 | tf_op jit(solution)/shard_map/ppermute | solution.py:266
  24.6 28.8 %copy-start.1 = (s32[1,1,2]{2,1,0:T(1,128)S(1)}, s32[1,1,2]{2,1,0:T(1,128)}, u32[]{:S(2)}) copy-start(s32[1,1,2]{2,1,0:T(1,128)} %param.11) | copy-start | bytes 28
  24.6 28.8 %copy-start.2 = (s32[1,1,2]{2,1,0:T(1,128)S(1)}, s32[1,1,2]{2,1,0:T(1,128)}, u32[]{:S(2)}) copy-start(s32[1,1,2]{2,1,0:T(1,128)} %param.12) | copy-start | bytes 28
  24.6 28.8 %copy-start.3 = (s32[1,3]{1,0:T(1,128)S(1)}, s32[1,3]{1,0:T(1,128)}, u32[]{:S(2)}) copy-start(s32[1,3]{1,0:T(1,128)} %param.13) | copy-start | bytes 40
  25.6 25.3 %all-to-all-start.1 = ((f32[16,6,16,128]{3,2,1,0:T(8,128)}), f32[16,6,16,128]{3,2,1,0:T(8,128)S(1)}, u32[]{:S(2)}, u32[]{:S(2)}) async-start(f32[16,6,16,128]{3,2,1,0:T(8,128)} %shard_map.96), calls=%async_computation.1 | async-start | bytes 1572864 | tf_op jit(solution)/shard_map/all_to_all | solution.py:227
  34.7 3.6 %collective-permute-start.2 = (f32[16,3,16,128]{3,2,1,0:T(8,128)S(1)}, f32[16,3,16,128]{3,2,1,0:T(8,128)S(1)}, u32[]{:S(2)}, u32[]{:S(2)}) collective-permute-start(f32[16,3,16,128]{3,2,1,0:T(8,128)S(1)} %all-to-all-done.unused.own_mine), channel_id=1, source_target_pairs={{0,32},{32,0},{1,33},{33,1},{2,34},{34,2},{3,35},{35,3},{4,36},{36... | collective-permute-start | bytes 1179656 | tf_op jit(solution)/shard_map/ppermute | solution.py:275
  50.8 4.2 %collective-permute-start.3 = (f32[16,6,16,128]{3,2,1,0:T(8,128)S(1)}, f32[16,6,16,128]{3,2,1,0:T(8,128)S(1)}, u32[]{:S(2)}, u32[]{:S(2)}) collective-permute-start(f32[16,6,16,128]{3,2,1,0:T(8,128)S(1)} %all-to-all-done.1.rim_mine), channel_id=1, source_target_pairs={{0,32},{32,0},{1,33},{33,1},{2,34},{34,2},{3,35},{35,3},{4,36},{36... | collective-permute-start | bytes 2359304 | tf_op jit(solution)/shard_map/ppermute | solution.py:278
  62.4 34.2 %collective-permute-start.4 = (f32[16,9,16,128]{3,2,1,0:T(8,128)}, f32[16,9,16,128]{3,2,1,0:T(8,128)S(1)}, u32[]{:S(2)}, u32[]{:S(2)}) collective-permute-start(f32[16,9,16,128]{3,2,1,0:T(8,128)} %get-tuple-element.19), channel_id=1, source_target_pairs={{0,32},{32,0},{1,33},{33,1},{2,34},{34,2},{3,35},{35,3},{4,36},{36... | collective-permute-start | bytes 3538952 | tf_op jit(solution)/shard_map/ppermute | solution.py:312
  78.3 32.3 %all-to-all-start.3 = ((f32[16,16,128]{2,1,0:T(8,128)}), f32[16,16,128]{2,1,0:T(8,128)S(1)}, u32[]{:S(2)}, u32[]{:S(2)}) async-start(f32[16,16,128]{2,1,0:T(8,128)} %shard_map.99), calls=%async_computation.3 | async-start | bytes 262144 | tf_op jit(solution)/shard_map/all_to_all | solution.py:227
  97.5 22.3 %collective-permute-start.5 = (f32[16,3,16,128]{3,2,1,0:T(8,128)}, f32[16,3,16,128]{3,2,1,0:T(8,128)S(1)}, u32[]{:S(2)}, u32[]{:S(2)}) collective-permute-start(f32[16,3,16,128]{3,2,1,0:T(8,128)} %get-tuple-element.21), channel_id=1, source_target_pairs={{0,1},{1,0},{2,3},{3,2},{4,5},{5,4},{6,7},{7,6},{8,9},{9,8},{10,11... | collective-permute-start | bytes 1179656 | tf_op jit(solution)/shard_map/ppermute | solution.py:323
  101.0 18.7 %collective-permute-start.6 = (f32[16,3,16,128]{3,2,1,0:T(8,128)S(1)}, f32[16,3,16,128]{3,2,1,0:T(8,128)S(1)}, u32[]{:S(2)}, u32[]{:S(2)}) collective-permute-start(f32[16,3,16,128]{3,2,1,0:T(8,128)S(1)} %get-tuple-element.22), channel_id=1, source_target_pairs={{1,2},{2,1},{3,4},{4,3},{5,6},{6,5},{7,8},{8,7},{9,10},{10,9},{11,... | collective-permute-start | bytes 1179656 | tf_op jit(solution)/shard_map/ppermute | solution.py:324
